TPU v7x, 32 devices: a whole 2x2x4 slice. The times are simulated.
32 devices in a mesh: dp: 8 (over z, y), seq: 4 (over x, core).
Axes of the slice: x: 2, y: 2, z: 4, core: 2. Of those that a mesh axis runs over, the one named last changes fastest.
Arguments:
- tokens: bfloat16 [16, 512, 768], P('dp', 'seq'), may hold values from -6 to 6
- lengths: int32 [16], P('dp'), may hold values from 64 to 512, as said below
- centre_flags: int32 [16, 512], P('dp', 'seq'), may hold values from 0 to 1
- cotangent: bfloat16 [16, 512, 768], P('dp', 'seq'), may hold values from -6 to 6
- mask_vector: float32 [768], replicated, may hold values from -6 to 6
- qkv_weight: bfloat16 [2, 768, 2304], replicated, may hold values from -0.21875 to 0.21875
- qv_bias: float32 [2, 1536], replicated, may hold values from -3 to 3
- out_weight: bfloat16 [2, 768, 768], replicated, may hold values from -0.875 to 0.875
- out_bias: float32 [2, 768], replicated, may hold values from -3 to 3
- attn_gain: float32 [2, 768], replicated, may hold values from 0.5 to 1.5
- attn_shift: float32 [2, 768], replicated, may hold values from -3 to 3
- up_weight: bfloat16 [2, 768, 3072], replicated, may hold values from -0.21875 to 0.21875
- up_bias: float32 [2, 3072], replicated, may hold values from -3 to 3
- down_weight: bfloat16 [2, 3072, 768], replicated, may hold values from -0.109375 to 0.109375
- down_bias: float32 [2, 768], replicated, may hold values from -3 to 3
- ffn_gain: float32 [2, 768], replicated, may hold values from 0.5 to 1.5
- ffn_shift: float32 [2, 768], replicated, may hold values from -3 to 3
Outputs:
- layer_out: float32 [16, 512, 768], P('dp', 'seq')
- input_grad: float32 [16, 512, 768], P('dp', 'seq')
- mask_vector_grad: float32 [768], P('dp')
- qkv_weight_grad: float32 [2, 768, 2304], P(None, 'dp')
- qv_bias_grad: float32 [2, 1536], P(None, 'dp')
- out_weight_grad: float32 [2, 768, 768], P(None, 'dp')
- out_bias_grad: float32 [2, 768], P(None, 'dp')
- attn_gain_grad: float32 [2, 768], P(None, 'dp')
- attn_shift_grad: float32 [2, 768], P(None, 'dp')
- up_weight_grad: float32 [2, 768, 3072], P(None, 'dp')
- up_bias_grad: float32 [2, 3072], P(None, 'dp')
- down_weight_grad: float32 [2, 3072, 768], P(None, 'dp')
- down_bias_grad: float32 [2, 768], P(None, 'dp')
- ffn_gain_grad: float32 [2, 768], P(None, 'dp')
- ffn_shift_grad: float32 [2, 768], P(None, 'dp')
Inputs may be any that keep to these rules, and one draw needn't show every extreme that they name: `lengths`: in each aligned block of 2 slots one slot has length 512 and another has length 64.
All inputs are finite; a program needn't handle non-finite values.
Results may differ from a plain program's by a relative error of at most 0.023.
Values may be sent and summed in bfloat16 or wider, within the bound.
No kernel may reach another device: no remote copies, remote signals or barrier semaphores. Data moves between devices by JAX's collectives and lax.ppermute only.
A program may use at most 256 MiB of HBM per device.

v0:
```python
import math

import jax
import jax.numpy as jnp
from jax import lax
from jax.sharding import PartitionSpec as P

HEADS = 12
SPAN = 5


NEG_FILL = -1000000000.0
LN_EPS = 1e-12
ROOT_HALF = 0.7071067811865476
INV_ROOT_TAU = 0.3989422804014327


def padded(cells, sides, width):
    for axis, dim in sides:
        count = lax.axis_size(axis)
        ends = count - 1
        head = lax.slice_in_dim(cells, 0, width, axis=dim)
        tail = lax.slice_in_dim(cells, cells.shape[dim] - width, cells.shape[dim], axis=dim)
        cells = jnp.concatenate(
            [
                lax.ppermute(tail, axis, [(i, (i + 1) % count) for i in range(ends)]),
                cells,
                lax.ppermute(head, axis, [((i + 1) % count, i) for i in range(ends)]),
            ],
            axis=dim,
        )
    return cells


def gelu_value(inputs):
    return 0.5 * inputs * (1.0 + lax.erf(inputs * ROOT_HALF))


def gelu_slope(inputs):
    return 0.5 * (1.0 + lax.erf(inputs * ROOT_HALF)) + inputs * INV_ROOT_TAU * jnp.exp(
        -0.5 * inputs * inputs
    )


def norm_forward(summed, gain, shift):
    centred = summed - jnp.mean(summed, axis=-1, keepdims=True)
    inverse = lax.rsqrt(jnp.mean(centred * centred, axis=-1, keepdims=True) + LN_EPS)
    normal_unit = centred * inverse
    return (normal_unit * gain + shift, normal_unit, inverse)


def norm_backward(upstream, normal_unit, inverse, gain):
    gain_grad = jnp.sum(upstream * normal_unit, axis=(0, 1))
    shift_grad = jnp.sum(upstream, axis=(0, 1))
    pushed = upstream * gain
    inner = (
        pushed
        - jnp.mean(pushed, axis=-1, keepdims=True)
        - normal_unit * jnp.mean(pushed * normal_unit, axis=-1, keepdims=True)
    )
    return (inner * inverse, gain_grad, shift_grad)


def project(inputs, weight):
    return jnp.einsum("std,dx->stx", inputs, weight, preferred_element_type=jnp.float32)


def project_back(upstream, weight):
    return jnp.einsum("stx,dx->std", upstream, weight, preferred_element_type=jnp.float32)


def contract_rows(inputs, upstream):
    return jnp.einsum("std,stx->dx", inputs, upstream, preferred_element_type=jnp.float32)


def split_heads(matrix):
    return matrix.reshape(matrix.shape[0], matrix.shape[1], HEADS, matrix.shape[2] // HEADS)


def score_block(queries, key_rows, keep_keys):
    query_heads = split_heads(queries)
    scaling = 1.0 / math.sqrt(query_heads.shape[3])
    raw_scores = (
        jnp.einsum(
            "sqhe,skhe->shqk",
            query_heads,
            split_heads(key_rows),
            preferred_element_type=jnp.float32,
        )
        * scaling
    )
    return (jnp.where(keep_keys[:, None, None, :], raw_scores, NEG_FILL), scaling)


def attend_forward(queries, key_rows, value_rows, keep_keys):
    scores, scaling = score_block(queries, key_rows, keep_keys)
    row_max = jnp.max(scores, axis=-1, keepdims=True)
    exp_scores = jnp.exp(scores - row_max)
    row_total = jnp.sum(exp_scores, axis=-1, keepdims=True)
    soft_low = (exp_scores / row_total).astype(jnp.bfloat16)
    mixed = jnp.einsum(
        "shqk,skhe->sqhe", soft_low, split_heads(value_rows), preferred_element_type=jnp.float32
    )
    return (mixed.reshape(queries.shape).astype(jnp.bfloat16), row_max + jnp.log(row_total))


def attend_backward(queries, key_rows, value_rows, keep_keys, log_total, context_grad):
    scores, scaling = score_block(queries, key_rows, keep_keys)
    soft_weights = jnp.exp(scores - log_total)
    grad_heads = split_heads(context_grad)
    value_grad = jnp.einsum(
        "shqk,sqhe->skhe",
        soft_weights.astype(jnp.bfloat16),
        grad_heads,
        preferred_element_type=jnp.float32,
    )
    weight_grad = jnp.einsum(
        "sqhe,skhe->shqk", grad_heads, split_heads(value_rows), preferred_element_type=jnp.float32
    )
    score_grad = (
        soft_weights * (weight_grad - jnp.sum(weight_grad * soft_weights, axis=-1, keepdims=True))
    ).astype(jnp.bfloat16)
    query_grad = (
        jnp.einsum(
            "shqk,skhe->sqhe", score_grad, split_heads(key_rows), preferred_element_type=jnp.float32
        )
        * scaling
    )
    key_grad = (
        jnp.einsum(
            "shqk,sqhe->skhe", score_grad, split_heads(queries), preferred_element_type=jnp.float32
        )
        * scaling
    )
    return (
        query_grad.reshape(queries.shape),
        key_grad.reshape(key_rows.shape),
        value_grad.reshape(value_rows.shape),
    )


def layer_forward(hidden, params, keep_keys):
    (
        qkv_weight,
        qv_bias,
        out_weight,
        out_bias,
        attn_gain,
        attn_shift,
        up_weight,
        up_bias,
        down_weight,
        down_bias,
        ffn_gain,
        ffn_shift,
    ) = params
    model_width = hidden.shape[2]
    inputs_low = hidden.astype(jnp.bfloat16)
    projected = project(inputs_low, qkv_weight)
    queries = (projected[..., :model_width] + qv_bias[:model_width]).astype(jnp.bfloat16)
    key_local = projected[..., model_width : 2 * model_width].astype(jnp.bfloat16)
    value_local = (projected[..., 2 * model_width :] + qv_bias[model_width:]).astype(jnp.bfloat16)
    key_rows, value_rows = (
        lax.all_gather(key_local, "seq", axis=1, tiled=True),
        lax.all_gather(value_local, "seq", axis=1, tiled=True),
    )
    context, log_total = attend_forward(queries, key_rows, value_rows, keep_keys)
    attended = project(context, out_weight) + out_bias
    normed, unit_one, inverse_one = norm_forward(hidden + attended, attn_gain, attn_shift)
    ffn_in = normed.astype(jnp.bfloat16)
    up_out = project(ffn_in, up_weight) + up_bias
    activated = gelu_value(up_out).astype(jnp.bfloat16)
    down_out = project(activated, down_weight) + down_bias
    output, unit_two, inverse_two = norm_forward(normed + down_out, ffn_gain, ffn_shift)
    saved_state = (
        inputs_low,
        queries,
        key_local,
        value_local,
        None,
        log_total,
        context,
        unit_one,
        inverse_one,
        ffn_in,
        up_out,
        activated,
        unit_two,
        inverse_two,
    )
    return (output, saved_state)


def layer_backward(upstream, params, saved_state, keep_keys):
    (
        qkv_weight,
        qv_bias,
        out_weight,
        out_bias,
        attn_gain,
        attn_shift,
        up_weight,
        up_bias,
        down_weight,
        down_bias,
        ffn_gain,
        ffn_shift,
    ) = params
    (
        inputs_low,
        queries,
        key_local,
        value_local,
        gathered,
        log_total,
        context,
        unit_one,
        inverse_one,
        ffn_in,
        up_out,
        activated,
        unit_two,
        inverse_two,
    ) = saved_state
    grad_two, ffn_gain_grad, ffn_shift_grad = norm_backward(
        upstream, unit_two, inverse_two, ffn_gain
    )
    down_low = grad_two.astype(jnp.bfloat16)
    down_weight_grad = contract_rows(activated, down_low)
    down_bias_grad = jnp.sum(down_low.astype(jnp.float32), axis=(0, 1))
    up_low = (project_back(down_low, down_weight) * gelu_slope(up_out)).astype(jnp.bfloat16)
    up_weight_grad = contract_rows(ffn_in, up_low)
    up_bias_grad = jnp.sum(up_low.astype(jnp.float32), axis=(0, 1))
    grad_normed = grad_two + project_back(up_low, up_weight)
    grad_mid, attn_gain_grad, attn_shift_grad = norm_backward(
        grad_normed, unit_one, inverse_one, attn_gain
    )
    attended_low = grad_mid.astype(jnp.bfloat16)
    out_weight_grad = contract_rows(context, attended_low)
    out_bias_grad = jnp.sum(attended_low.astype(jnp.float32), axis=(0, 1))
    context_grad = project_back(attended_low, out_weight).astype(jnp.bfloat16)
    key_rows, value_rows = (
        lax.all_gather(key_local, "seq", axis=1, tiled=True),
        lax.all_gather(value_local, "seq", axis=1, tiled=True),
    )
    query_grad, key_part, value_part = attend_backward(
        queries, key_rows, value_rows, keep_keys, log_total, context_grad
    )
    key_grad, value_grad = (
        lax.psum_scatter(
            key_part.astype(jnp.bfloat16), "seq", scatter_dimension=1, tiled=True
        ).astype(jnp.float32),
        lax.psum_scatter(
            value_part.astype(jnp.bfloat16), "seq", scatter_dimension=1, tiled=True
        ).astype(jnp.float32),
    )
    query_low = query_grad.astype(jnp.bfloat16)
    value_low = value_grad.astype(jnp.bfloat16)
    proj_grad = jnp.concatenate([query_low, key_grad.astype(jnp.bfloat16), value_low], axis=-1)
    qkv_weight_grad = contract_rows(inputs_low, proj_grad)
    qv_bias_grad = jnp.concatenate(
        [
            jnp.sum(query_low.astype(jnp.float32), axis=(0, 1)),
            jnp.sum(value_low.astype(jnp.float32), axis=(0, 1)),
        ]
    )
    grad_hidden = grad_mid + project_back(proj_grad, qkv_weight)
    weight_terms = (
        qkv_weight_grad,
        qv_bias_grad,
        out_weight_grad,
        out_bias_grad,
        attn_gain_grad,
        attn_shift_grad,
        up_weight_grad,
        up_bias_grad,
        down_weight_grad,
        down_bias_grad,
        ffn_gain_grad,
        ffn_shift_grad,
    )
    return (grad_hidden, weight_terms)


def per_device(
    tokens,
    lengths,
    centre_flags,
    cotangent,
    mask_vector,
    qkv_weight,
    qv_bias,
    out_weight,
    out_bias,
    attn_gain,
    attn_shift,
    up_weight,
    up_bias,
    down_weight,
    down_bias,
    ffn_gain,
    ffn_shift,
):
    row_count = tokens.shape[1]
    widened = padded(centre_flags, (("seq", 1),), SPAN)
    centre_count = widened[:, 0:row_count]
    for offset in range(1, 2 * SPAN + 1):
        centre_count = centre_count + widened[:, offset : offset + row_count]
    masked = (centre_count > 0).astype(jnp.float32)[:, :, None]
    keep_keys = (
        jnp.arange(row_count * lax.axis_size("seq"), dtype=jnp.int32)[None, :] < lengths[:, None]
    )
    hidden = tokens.astype(jnp.float32) * (1.0 - masked) + masked * mask_vector
    all_params = (
        qkv_weight,
        qv_bias,
        out_weight,
        out_bias,
        attn_gain,
        attn_shift,
        up_weight,
        up_bias,
        down_weight,
        down_bias,
        ffn_gain,
        ffn_shift,
    )
    layer_count = qkv_weight.shape[0]
    saved_states = []
    for layer_index in range(layer_count):
        hidden, saved_state = layer_forward(
            hidden, tuple((weight[layer_index] for weight in all_params)), keep_keys
        )
        saved_states.append(saved_state)
    upstream = cotangent.astype(jnp.float32)
    collected = [None] * layer_count
    for layer_index in reversed(range(layer_count)):
        upstream, terms = layer_backward(
            upstream,
            tuple((weight[layer_index] for weight in all_params)),
            saved_states[layer_index],
            keep_keys,
        )
        if layer_index == 0:
            input_grad = upstream * (1.0 - masked)
            mask_term = jnp.sum(upstream * masked, axis=(0, 1))
        collected[layer_index] = terms
    stacked = [
        jnp.stack([collected[layer_index][position] for layer_index in range(layer_count)])
        for position in range(12)
    ]
    reduced = (
        lax.psum_scatter(stacked[0], "dp", scatter_dimension=1, tiled=True),
        lax.psum_scatter(stacked[1], "dp", scatter_dimension=1, tiled=True),
        lax.psum_scatter(stacked[2], "dp", scatter_dimension=1, tiled=True),
        lax.psum_scatter(stacked[3], "dp", scatter_dimension=1, tiled=True),
        lax.psum_scatter(stacked[4], "dp", scatter_dimension=1, tiled=True),
        lax.psum_scatter(stacked[5], "dp", scatter_dimension=1, tiled=True),
        lax.psum_scatter(stacked[6], "dp", scatter_dimension=1, tiled=True),
        lax.psum_scatter(stacked[7], "dp", scatter_dimension=1, tiled=True),
        lax.psum_scatter(stacked[8], "dp", scatter_dimension=1, tiled=True),
        lax.psum_scatter(stacked[9], "dp", scatter_dimension=1, tiled=True),
        lax.psum_scatter(stacked[10], "dp", scatter_dimension=1, tiled=True),
        lax.psum_scatter(stacked[11], "dp", scatter_dimension=1, tiled=True),
        lax.psum_scatter(mask_term[None, :], "dp", scatter_dimension=1, tiled=True),
    )
    shares = list(reduced[:12]) + [reduced[12][0]]
    summed = (
        lax.psum(shares[0].astype(jnp.bfloat16), "seq").astype(jnp.float32),
        lax.psum(shares[1].astype(jnp.bfloat16), "seq").astype(jnp.float32),
        lax.psum(shares[2].astype(jnp.bfloat16), "seq").astype(jnp.float32),
        lax.psum(shares[3].astype(jnp.bfloat16), "seq").astype(jnp.float32),
        lax.psum(shares[4].astype(jnp.bfloat16), "seq").astype(jnp.float32),
        lax.psum(shares[5].astype(jnp.bfloat16), "seq").astype(jnp.float32),
        lax.psum(shares[6].astype(jnp.bfloat16), "seq").astype(jnp.float32),
        lax.psum(shares[7].astype(jnp.bfloat16), "seq").astype(jnp.float32),
        lax.psum(shares[8].astype(jnp.bfloat16), "seq").astype(jnp.float32),
        lax.psum(shares[9].astype(jnp.bfloat16), "seq").astype(jnp.float32),
        lax.psum(shares[10].astype(jnp.bfloat16), "seq").astype(jnp.float32),
        lax.psum(shares[11].astype(jnp.bfloat16), "seq").astype(jnp.float32),
        lax.psum(shares[12].astype(jnp.bfloat16), "seq").astype(jnp.float32),
    )
    return (
        hidden,
        input_grad,
        summed[12],
        summed[0],
        summed[1],
        summed[2],
        summed[3],
        summed[4],
        summed[5],
        summed[6],
        summed[7],
        summed[8],
        summed[9],
        summed[10],
        summed[11],
    )


def solution(mesh):
    placed = (
        P("dp", "seq", None),
        P("dp"),
        P("dp", "seq"),
        P("dp", "seq", None),
        P(),
        P(),
        P(),
        P(),
        P(),
        P(),
        P(),
        P(),
        P(),
        P(),
        P(),
        P(),
        P(),
    )
    return jax.shard_map(
        per_device,
        mesh=mesh,
        in_specs=placed,
        out_specs=(
            P("dp", "seq", None),
            P("dp", "seq", None),
            P("dp"),
            P(None, "dp", None),
            P(None, "dp"),
            P(None, "dp", None),
            P(None, "dp"),
            P(None, "dp"),
            P(None, "dp"),
            P(None, "dp", None),
            P(None, "dp"),
            P(None, "dp", None),
            P(None, "dp"),
            P(None, "dp"),
            P(None, "dp"),
        ),
        check_vma=False,
    )
```

profile of v0, /device:TPU:0, one launch (start us, length us, event | category | flops | bytes accessed | tf_op | source)
XLA Modules:
  0.0 1930.9 jit_solution(1339723792147461134)
XLA Ops:
  23.4 19.2 all-gather.7.cloned.1.call-done
  49.7 14.7 all-gather.5.cloned.1.call-done
  66.3 4.5 fusion.107
  86.1 17.2 all-gather.11.cloned.1.call-done
  110.6 14.4 all-gather.9.cloned.1.call-done
  154.6 4.9 multiply_reduce_fusion.1
  174.3 8.5 reduce-scatter.38.cloned.1.call-done
  182.8 31.3 %reduce-scatter.36.cloned.1.call-done = bf16[2,128,768]{2,1,0:T(8,128)(2,1)} async-done(((bf16[2,512,768]{2,1,0:T(8,128)(2,1)}), bf16[2,128,768]{2,1,0:T(8,128)(2,1)}) %reduce-scatter.36.cloned.1.call-update) | async-done | bytes 393232 | tf_op jit(solution)/shard_map/reduce_scatter | solution.py:250
  214.2 5.1 multiply_reduce_fusion.2
  220.2 4.6 convert_reduce_fusion.1
  236.5 4.9 multiply_reduce_fusion
  259.5 5.7 convolution_bitcast_fusion.4
  265.3 30.7 %reduce-scatter.40.cloned.1.call-done = bf16[2,128,768]{2,1,0:T(8,128)(2,1)} async-done(((bf16[2,512,768]{2,1,0:T(8,128)(2,1)}), bf16[2,128,768]{2,1,0:T(8,128)(2,1)}) %reduce-scatter.40.cloned.1.call-update) | async-done | bytes 393232 | tf_op jit(solution)/shard_map/reduce_scatter | solution.py:250
  296.0 5.3 convolution_bitcast_fusion.5
  301.3 11.0 pad_maximum_fusion.2
  318.0 6.9 pad_maximum_fusion
  330.4 6.8 pad_maximum_fusion.1
  353.1 41.8 %reduce-scatter.46.cloned.1.call-done = f32[2,96,768]{2,1,0:T(8,128)} async-done(((f32[2,768,768]{2,1,0:T(8,128)}), f32[2,96,768]{2,1,0:T(8,128)}) %reduce-scatter.46.cloned.1.call-update) | async-done | bytes 589840 | tf_op jit(solution)/shard_map/reduce_scatter | solution.py:355
  396.8 230.6 %reduce-scatter.44.cloned.1.call-done = f32[2,96,2304]{2,1,0:T(8,128)} async-done(((f32[2,768,2304]{2,1,0:T(8,128)}), f32[2,96,2304]{2,1,0:T(8,128)}) %reduce-scatter.44.cloned.1.call-update) | async-done | bytes 1769488 | tf_op jit(solution)/shard_map/reduce_scatter | solution.py:353
  629.9 313.8 %reduce-scatter.48.cloned.1.call-done = f32[2,96,3072]{2,1,0:T(8,128)} async-done(((f32[2,768,3072]{2,1,0:T(8,128)}), f32[2,96,3072]{2,1,0:T(8,128)}) %reduce-scatter.48.cloned.1.call-update) | async-done | bytes 2359312 | tf_op jit(solution)/shard_map/reduce_scatter | solution.py:359
  946.6 312.8 %reduce-scatter.50.cloned.1.call-done = f32[2,384,768]{2,1,0:T(8,128)} async-done(((f32[2,3072,768]{2,1,0:T(8,128)}), f32[2,384,768]{2,1,0:T(8,128)}) %reduce-scatter.50.cloned.1.call-update) | async-done | bytes 2359312 | tf_op jit(solution)/shard_map/reduce_scatter | solution.py:361
  1262.2 61.0 %reduce-scatter.56.cloned.1.call-done = f32[96,2]{1,0:T(8,128)} async-done(((f32[768,2]{1,0:T(8,128)}), f32[96,2]{1,0:T(8,128)}) %reduce-scatter.56.cloned.1.call-update) | async-done | bytes 784
  1324.1 62.6 %reduce-scatter.58.cloned.1.call-done = f32[96,2]{1,0:T(8,128)} async-done(((f32[768,2]{1,0:T(8,128)}), f32[96,2]{1,0:T(8,128)}) %reduce-scatter.58.cloned.1.call-update) | async-done | bytes 784
  1387.6 62.6 %reduce-scatter.60.cloned.1.call-done = f32[96,2]{1,0:T(8,128)} async-done(((f32[768,2]{1,0:T(8,128)}), f32[96,2]{1,0:T(8,128)}) %reduce-scatter.60.cloned.1.call-update) | async-done | bytes 784
  1451.1 62.7 %reduce-scatter.64.cloned.1.call-done = f32[96,2]{1,0:T(8,128)} async-done(((f32[768,2]{1,0:T(8,128)}), f32[96,2]{1,0:T(8,128)}) %reduce-scatter.64.cloned.1.call-update) | async-done | bytes 784
  1514.7 62.6 %reduce-scatter.66.cloned.1.call-done = f32[96,2]{1,0:T(8,128)} async-done(((f32[768,2]{1,0:T(8,128)}), f32[96,2]{1,0:T(8,128)}) %reduce-scatter.66.cloned.1.call-update) | async-done | bytes 784
  1578.1 62.7 %reduce-scatter.68.cloned.1.call-done = f32[96,2]{1,0:T(8,128)} async-done(((f32[768,2]{1,0:T(8,128)}), f32[96,2]{1,0:T(8,128)}) %reduce-scatter.68.cloned.1.call-update) | async-done | bytes 784
  1641.7 67.0 %reduce-scatter.62.cloned.1.call-done = f32[384,2]{1,0:T(8,128)} async-done(((f32[3072,2]{1,0:T(8,128)}), f32[384,2]{1,0:T(8,128)}) %reduce-scatter.62.cloned.1.call-update) | async-done | bytes 3088
  1709.7 63.3 %reduce-scatter.52.cloned.1.call-done = f32[96,1]{1,0:T(8,128)} async-done(((f32[768,1]{1,0:T(8,128)}), f32[96,1]{1,0:T(8,128)}) %reduce-scatter.52.cloned.1.call-update) | async-done | bytes 400
  1774.0 64.3 %reduce-scatter.54.cloned.1.call-done = f32[192,2]{1,0:T(8,128)} async-done(((f32[1536,2]{1,0:T(8,128)}), f32[192,2]{1,0:T(8,128)}) %reduce-scatter.54.cloned.1.call-update) | async-done | bytes 1552
  1839.2 5.7 all-reduce
  1850.0 65.9 %all-reduce.4.cloned.1.call-done = (bf16[2,96,2304]{2,1,0:T(8,128)(2,1)}, bf16[2,96,768]{2,1,0:T(8,128)(2,1)}, bf16[2,96,3072]{2,1,0:T(8,128)(2,1)}, bf16[2,384,768]{2,1,0:T(8,128)(2,1)}) async-done(((bf16[2,96,2304]{2,1,0:T(8,128)(2,1)}, bf16[2,96,768]{2,1,0:T(8,128)(2,1)}, bf16[2,96,3072]{2,1,0:T(8,128)(2,1)}, bf16[2,384,768]{2,1,0:T(8,128)(2,1)}), (bf16[2,96,2304]{2,1,0:T(8,128)(2,1)}, ...) | async-done | bytes 3538960 | tf_op jit(solution)/shard_map/psum | solution.py:369
  (495 shorter events, 178.8 us)
Async XLA Ops:
  7.2 35.4 %all-gather.7.cloned.1.call-start = ((), (), s32[]{:S(2)}) async-start(), calls=%async_computation.18 | async-start | bytes 1966080 | tf_op jit(solution)/shard_map/all_gather | solution.py:164
  8.1 5.0 collective-permute-start.1
  9.3 3.8 collective-permute-start
  14.2 56.6 %copy-start.80 = (f32[2,128]{1,0:T(2,128)}, f32[2,128]{1,0:T(2,128)S(1)}, u32[]{:S(2)}) copy-start(f32[2,128]{1,0:T(2,128)S(1)} %get-tuple-element.68) | copy-start | bytes 3076
  14.2 56.6 %copy-start.83 = (f32[2,128]{1,0:T(2,128)}, f32[2,128]{1,0:T(2,128)S(1)}, u32[]{:S(2)}) copy-start(f32[2,128]{1,0:T(2,128)S(1)} %get-tuple-element.69) | copy-start | bytes 3076
  18.4 46.0 %all-gather.5.cloned.1.call-start = ((), (), s32[]{:S(2)}) async-start(), calls=%async_computation.17 | async-start | bytes 1966080 | tf_op jit(solution)/shard_map/all_gather | solution.py:165
  20.0 83.3 %all-gather.11.cloned.1.call-start = ((), (), s32[]{:S(2)}) async-start(), calls=%async_computation.20 | async-start | bytes 1966080 | tf_op jit(solution)/shard_map/all_gather | solution.py:164
  21.9 55.0 %copy-start.59 = (f32[768]{0:T(1024)}, f32[768]{0:T(1024)S(1)}, u32[]{:S(2)}) copy-start(f32[768]{0:T(1024)S(1)} %get-tuple-element.44) | copy-start | bytes 9220
  79.0 51.9 %copy-start.4 = (f32[2,128,768]{2,1,0:T(8,128)}, f32[2,128,768]{2,1,0:T(8,128)S(1)}, u32[]{:S(2)}) copy-start(f32[2,128,768]{2,1,0:T(8,128)S(1)} %get-tuple-element.88) | copy-start | bytes 2359300
  83.5 41.5 %all-gather.9.cloned.1.call-start = ((), (), s32[]{:S(2)}) async-start(), calls=%async_computation.19 | async-start | bytes 1966080 | tf_op jit(solution)/shard_map/all_gather | solution.py:165
  85.8 97.0 %reduce-scatter.38.cloned.1.call-start = ((), (), s32[]{:S(2)}) async-start(), calls=%async_computation.22 | async-start | bytes 1966080 | tf_op jit(solution)/shard_map/reduce_scatter | solution.py:253
  154.5 59.7 %reduce-scatter.36.cloned.1.call-start = ((), (), s32[]{:S(2)}) async-start(), calls=%async_computation.21 | async-start | bytes 1966080 | tf_op jit(solution)/shard_map/reduce_scatter | solution.py:250
  167.8 97.5 %reduce-scatter.42.cloned.1.call-start = ((), (), s32[]{:S(2)}) async-start(), calls=%async_computation.24 | async-start | bytes 1966080 | tf_op jit(solution)/shard_map/reduce_scatter | solution.py:253
  174.3 45.0 %copy-start.28 = (bf16[2,128,768]{2,1,0:T(8,128)(2,1)}, bf16[2,128,768]{2,1,0:T(8,128)(2,1)S(1)}, u32[]{:S(2)}) copy-start(bf16[2,128,768]{2,1,0:T(8,128)(2,1)S(1)} %copy.95) | copy-start | bytes 1179652
  174.3 45.0 %copy-start.5 = (f32[2,128,768]{2,1,0:T(8,128)S(1)}, f32[2,128,768]{2,1,0:T(8,128)}, u32[]{:S(2)}) copy-start(f32[2,128,768]{2,1,0:T(8,128)} %copy-done.4) | copy-start | bytes 2359300
  174.3 44.9 %copy-start.67 = (f32[2,128]{1,0:T(2,128)S(1)}, f32[2,128]{1,0:T(2,128)}, u32[]{:S(2)}) copy-start(f32[2,128]{1,0:T(2,128)} %copy-done.65) | copy-start | bytes 3076
  174.3 44.9 %copy-start.70 = (f32[2,128]{1,0:T(2,128)S(1)}, f32[2,128]{1,0:T(2,128)}, u32[]{:S(2)}) copy-start(f32[2,128]{1,0:T(2,128)} %copy-done.68) | copy-start | bytes 3076
  236.2 59.8 %reduce-scatter.40.cloned.1.call-start = ((), (), s32[]{:S(2)}) async-start(), calls=%async_computation.23 | async-start | bytes 1966080 | tf_op jit(solution)/shard_map/reduce_scatter | solution.py:250
  249.7 145.2 %reduce-scatter.46.cloned.1.call-start = ((), (), s32[]{:S(2)}) async-start(), calls=%async_computation.26 | async-start | bytes 5308416 | tf_op jit(solution)/shard_map/reduce_scatter | solution.py:355
  254.3 373.1 %reduce-scatter.44.cloned.1.call-start = ((), (), s32[]{:S(2)}) async-start(), calls=%async_computation.25 | async-start | bytes 15925248 | tf_op jit(solution)/shard_map/reduce_scatter | solution.py:353
  312.4 631.4 %reduce-scatter.48.cloned.1.call-start = ((), (), s32[]{:S(2)}) async-start(), calls=%async_computation.27 | async-start | bytes 21233664 | tf_op jit(solution)/shard_map/reduce_scatter | solution.py:359
  325.0 934.4 %reduce-scatter.50.cloned.1.call-start = ((), (), s32[]{:S(2)}) async-start(), calls=%async_computation.28 | async-start | bytes 21233664 | tf_op jit(solution)/shard_map/reduce_scatter | solution.py:361
  337.4 985.9 %reduce-scatter.56.cloned.1.call-start = ((), (), s32[]{:S(2)}) async-start(), calls=%async_computation.31 | async-start | bytes 442368
  339.1 1047.6 %reduce-scatter.58.cloned.1.call-start = ((), (), s32[]{:S(2)}) async-start(), calls=%async_computation.32 | async-start | bytes 442368
  340.2 1110.1 %reduce-scatter.60.cloned.1.call-start = ((), (), s32[]{:S(2)}) async-start(), calls=%async_computation.33 | async-start | bytes 442368
  341.3 1172.5 %reduce-scatter.64.cloned.1.call-start = ((), (), s32[]{:S(2)}) async-start(), calls=%async_computation.35 | async-start | bytes 442368
  342.4 1234.9 %reduce-scatter.66.cloned.1.call-start = ((), (), s32[]{:S(2)}) async-start(), calls=%async_computation.36 | async-start | bytes 442368
  343.5 1297.3 %reduce-scatter.68.cloned.1.call-start = ((), (), s32[]{:S(2)}) async-start(), calls=%async_computation.37 | async-start | bytes 442368
  344.5 1364.2 %reduce-scatter.62.cloned.1.call-start = ((), (), s32[]{:S(2)}) async-start(), calls=%async_computation.34 | async-start | bytes 1769472
  346.4 1426.6 %reduce-scatter.52.cloned.1.call-start = ((), (), s32[]{:S(2)}) async-start(), calls=%async_computation.29 | async-start | bytes 442368
  351.8 1486.5 %reduce-scatter.54.cloned.1.call-start = ((), (), s32[]{:S(2)}) async-start(), calls=%async_computation.30 | async-start | bytes 884736
  353.1 1562.8 %all-reduce.4.cloned.1.call-start = ((), (), s32[]{:S(2)}) async-start(), calls=%async_computation.38 | async-start | bytes 7077888 | tf_op jit(solution)/shard_map/psum | solution.py:369
  (135 other events, 750.5 us)
Sparse Core Ops, SparseCore 0:
  18.5 24.0 all-gather.6
  44.7 19.6 all-gather.4
  83.6 19.6 all-gather.10
  105.3 19.6 all-gather.8
  154.6 28.1 reduce-scatter.37
  186.0 28.1 reduce-scatter.35
  236.3 28.1 reduce-scatter.41
  267.8 28.1 reduce-scatter.39
  299.6 95.2 reduce-scatter.45
  398.4 228.9 reduce-scatter.43
  631.3 312.4 reduce-scatter.47
  947.5 311.8 reduce-scatter.49
  1262.7 60.5 reduce-scatter.55
  1326.3 60.3 reduce-scatter.57
  1389.8 60.3 reduce-scatter.59
  1453.3 60.3 reduce-scatter.63
  1516.9 60.3 reduce-scatter.65
  1580.4 60.3 reduce-scatter.67
  1644.8 63.8 reduce-scatter.61
  1712.8 60.2 reduce-scatter.51
  1776.7 61.4 reduce-scatter.53
  1841.4 74.4 all-reduce.3
where the time goes:
time: 1940 us; the launch traced here: 1930 us
  waiting for transfers between devices  1670 us (86%)
  matrix products  98.8 us (5%)
  other arithmetic  74.5 us (4%)
  local copies, waits for them, and re-layouts  59 us (3%)
    unnamed x31, waiting for transfers between devices  569 us
    reduce_scatter x1, waiting for transfers between devices, per_device(): lax.psum_scatter(stacked[6], 'dp', scatter_dimension=1, tiled=True)  314 us
    reduce_scatter x1, waiting for transfers between devices, per_device(): lax.psum_scatter(stacked[8], 'dp', scatter_dimension=1, tiled=True)  313 us
    reduce_scatter x1, waiting for transfers between devices, per_device(): lax.psum_scatter(stacked[0], 'dp', scatter_dimension=1, tiled=True)  231 us
    psum x1, waiting for transfers between devices, per_device(): lax.psum(shares[0].astype(jnp.bfloat16), 'seq').astype(jnp.float32)  65.9 us
    reduce_scatter x2, waiting for transfers between devices, layer_backward(): lax.psum_scatter(key_part.astype(jnp.bfloat16), 'seq', scatter_dimension=...  62.1 us
    reduce_scatter x1, waiting for transfers between devices, per_device(): lax.psum_scatter(stacked[2], 'dp', scatter_dimension=1, tiled=True)  41.8 us
  transfers between devices with their start and end apart: 24, of which 22 were waited for; matrix products, arithmetic and copies ran while one was open for 7% of the time, Pallas kernels for 0%

commit v1 on v0

v1 whole, which is shorter than its diff:
```python
import math

import jax
import jax.numpy as jnp
from jax import lax
from jax.sharding import PartitionSpec as P

HEADS = 12
SPAN = 5

NEG_FILL = -1000000000.0
LN_EPS = 1e-12
ROOT_HALF = 0.7071067811865476
INV_ROOT_TAU = 0.3989422804014327

F32 = jnp.float32
BF16 = jnp.bfloat16


def swap_seq(value, bit):
    count = lax.axis_size("seq")
    return lax.ppermute(value, "seq", [(i, i ^ bit) for i in range(count)])


def swap_dp(value, bit):
    count = lax.axis_size("dp")
    return lax.ppermute(value, "dp", [(i, i ^ bit) for i in range(count)])


def gelu_value(inputs):
    return 0.5 * inputs * (1.0 + lax.erf(inputs * ROOT_HALF))


def gelu_slope(inputs):
    return 0.5 * (1.0 + lax.erf(inputs * ROOT_HALF)) + inputs * INV_ROOT_TAU * jnp.exp(
        -0.5 * inputs * inputs
    )


def norm_forward(summed, gain, shift):
    centred = summed - jnp.mean(summed, axis=-1, keepdims=True)
    inverse = lax.rsqrt(jnp.mean(centred * centred, axis=-1, keepdims=True) + LN_EPS)
    unit = centred * inverse
    return unit * gain + shift, unit, inverse


def norm_backward(upstream, unit, inverse, gain):
    gain_grad = jnp.sum(upstream * unit, axis=0)
    shift_grad = jnp.sum(upstream, axis=0)
    pushed = upstream * gain
    inner = (
        pushed
        - jnp.mean(pushed, axis=-1, keepdims=True)
        - unit * jnp.mean(pushed * unit, axis=-1, keepdims=True)
    )
    return inner * inverse, gain_grad, shift_grad


def dot(a, b):
    return lax.dot_general(a, b, (((1,), (0,)), ((), ())), preferred_element_type=F32)


def dot_bt(a, b):
    return lax.dot_general(a, b, (((1,), (1,)), ((), ())), preferred_element_type=F32)


def dot_at(a, b):
    return lax.dot_general(a, b, (((0,), (0,)), ((), ())), preferred_element_type=F32)


def heads_of(matrix):
    return matrix.reshape(matrix.shape[0], HEADS, matrix.shape[1] // HEADS)


def attend_forward(queries, key_rows, value_rows, keep):
    q, k, v = heads_of(queries), heads_of(key_rows), heads_of(value_rows)
    scaling = 1.0 / math.sqrt(q.shape[2])
    scores = jnp.einsum("qhe,khe->hqk", q, k, preferred_element_type=F32) * scaling
    scores = jnp.where(keep[None, None, :], scores, NEG_FILL)
    row_max = jnp.max(scores, axis=-1, keepdims=True)
    exp_scores = jnp.exp(scores - row_max)
    row_total = jnp.sum(exp_scores, axis=-1, keepdims=True)
    low = (exp_scores / row_total).astype(BF16)
    mixed = jnp.einsum("hqk,khe->qhe", low, v, preferred_element_type=F32)
    return mixed.reshape(queries.shape).astype(BF16), row_max + jnp.log(row_total)


def attend_backward(queries, key_rows, value_rows, keep, log_total, context_grad):
    q, k, v, g = heads_of(queries), heads_of(key_rows), heads_of(value_rows), heads_of(context_grad)
    scaling = 1.0 / math.sqrt(q.shape[2])
    scores = jnp.einsum("qhe,khe->hqk", q, k, preferred_element_type=F32) * scaling
    scores = jnp.where(keep[None, None, :], scores, NEG_FILL)
    soft = jnp.exp(scores - log_total)
    value_grad = jnp.einsum("hqk,qhe->khe", soft.astype(BF16), g, preferred_element_type=F32)
    prob_grad = jnp.einsum("qhe,khe->hqk", g, v, preferred_element_type=F32)
    inner = jnp.sum(prob_grad * soft, axis=-1, keepdims=True)
    score_grad = (soft * (prob_grad - inner)).astype(BF16)
    query_grad = jnp.einsum("hqk,khe->qhe", score_grad, k, preferred_element_type=F32) * scaling
    key_grad = jnp.einsum("hqk,qhe->khe", score_grad, q, preferred_element_type=F32) * scaling
    return (
        query_grad.reshape(queries.shape),
        key_grad.reshape(key_rows.shape),
        value_grad.reshape(value_rows.shape),
    )


def both(own):
    return jnp.concatenate([own, swap_seq(own, 1)], axis=0)


def layer_forward(hidden, params, keep):
    (
        qkv_weight, qv_bias, out_weight, out_bias, attn_gain, attn_shift,
        up_weight, up_bias, down_weight, down_bias, ffn_gain, ffn_shift,
    ) = params
    width = hidden.shape[1]
    inputs_low = hidden.astype(BF16)
    projected = dot(inputs_low, qkv_weight)
    queries = (projected[:, :width] + qv_bias[:width]).astype(BF16)
    key_own = projected[:, width : 2 * width].astype(BF16)
    value_own = (projected[:, 2 * width :] + qv_bias[width:]).astype(BF16)
    key_rows, value_rows = both(key_own), both(value_own)
    context, log_total = attend_forward(queries, key_rows, value_rows, keep)
    attended = dot(context, out_weight) + out_bias
    normed, unit_one, inverse_one = norm_forward(hidden + attended, attn_gain, attn_shift)
    ffn_in = normed.astype(BF16)
    up_out = dot(ffn_in, up_weight) + up_bias
    activated = gelu_value(up_out).astype(BF16)
    down_out = dot(activated, down_weight) + down_bias
    output, unit_two, inverse_two = norm_forward(normed + down_out, ffn_gain, ffn_shift)
    saved = (
        inputs_low, queries, key_rows, value_rows, log_total, context, unit_one, inverse_one,
        ffn_in, up_out, activated, unit_two, inverse_two,
    )
    return output, saved


def half_columns(matrix, index):
    half = matrix.shape[1] // 2
    return lax.dynamic_slice_in_dim(matrix, index * half, half, axis=1)


def weight_grad(inputs_both, upstream, core):
    own = half_columns(upstream, core)
    other = swap_seq(half_columns(upstream, 1 - core), 1)
    return dot_at(inputs_both, jnp.concatenate([own, other], axis=0)).astype(BF16)


def layer_backward(upstream, params, saved, keep, core):
    (
        qkv_weight, qv_bias, out_weight, out_bias, attn_gain, attn_shift,
        up_weight, up_bias, down_weight, down_bias, ffn_gain, ffn_shift,
    ) = params
    (
        inputs_low, queries, key_rows, value_rows, log_total, context, unit_one, inverse_one,
        ffn_in, up_out, activated, unit_two, inverse_two,
    ) = saved
    rows = upstream.shape[0]
    grad_two, ffn_gain_grad, ffn_shift_grad = norm_backward(upstream, unit_two, inverse_two, ffn_gain)
    down_low = grad_two.astype(BF16)
    down_weight_grad = weight_grad(both(activated), down_low, core)
    down_bias_grad = jnp.sum(down_low.astype(F32), axis=0)
    up_low = (dot_bt(down_low, down_weight) * gelu_slope(up_out)).astype(BF16)
    up_weight_grad = weight_grad(both(ffn_in), up_low, core)
    up_bias_grad = jnp.sum(up_low.astype(F32), axis=0)
    grad_normed = grad_two + dot_bt(up_low, up_weight)
    grad_mid, attn_gain_grad, attn_shift_grad = norm_backward(grad_normed, unit_one, inverse_one, attn_gain)
    attended_low = grad_mid.astype(BF16)
    out_weight_grad = weight_grad(both(context), attended_low, core)
    out_bias_grad = jnp.sum(attended_low.astype(F32), axis=0)
    context_grad = dot_bt(attended_low, out_weight).astype(BF16)
    query_grad, key_part, value_part = attend_backward(
        queries, key_rows, value_rows, keep, log_total, context_grad
    )
    key_grad = key_part[:rows] + swap_seq(key_part[rows:].astype(BF16), 1).astype(F32)
    value_grad = value_part[:rows] + swap_seq(value_part[rows:].astype(BF16), 1).astype(F32)
    query_low, value_low = query_grad.astype(BF16), value_grad.astype(BF16)
    proj_grad = jnp.concatenate([query_low, key_grad.astype(BF16), value_low], axis=1)
    qkv_weight_grad = weight_grad(both(inputs_low), proj_grad, core)
    qv_bias_grad = jnp.concatenate(
        [jnp.sum(query_low.astype(F32), axis=0), jnp.sum(value_low.astype(F32), axis=0)]
    )
    grad_hidden = grad_mid + dot_bt(proj_grad, qkv_weight)
    matrices = (qkv_weight_grad, out_weight_grad, up_weight_grad, down_weight_grad)
    vectors = (
        qv_bias_grad, out_bias_grad, attn_gain_grad, attn_shift_grad,
        up_bias_grad, down_bias_grad, ffn_gain_grad, ffn_shift_grad,
    )
    return grad_hidden, matrices, vectors


def halve(block, axis, mine, swap):
    sent = lax.dynamic_index_in_dim(block, 1 - mine, axis, keepdims=False)
    kept = lax.dynamic_index_in_dim(block, mine, axis, keepdims=False)
    return (kept.astype(F32) + swap(sent).astype(F32)).astype(BF16)


def scatter_sum(matrix, place, x_first):
    dp = lax.axis_size("dp")
    x, dp_index = place
    bits = dp.bit_length() - 1
    share = matrix.shape[0] // dp // 2
    block = matrix.reshape((2,) * (bits + 1) + (share, matrix.shape[1]))
    low_bit = lambda b, axis: halve(b, axis, dp_index & 1, lambda v: swap_dp(v, 1))
    x_step = lambda b, axis: halve(b, axis, x, lambda v: swap_seq(v, 2))
    if x_first:
        block = x_step(block, bits)
        block = low_bit(block, bits - 1)
    else:
        block = low_bit(block, bits - 1)
        block = x_step(block, bits - 1)
    for bit in range(1, bits):
        axis = bits - 1 - bit
        block = halve(block, axis, (dp_index >> bit) & 1, lambda v, bit=bit: swap_dp(v, 1 << bit))
    return block


def gather_share(block, x, core):
    other = swap_seq(block, 2)
    rows = jnp.where(x == 0, jnp.concatenate([block, other]), jnp.concatenate([other, block]))
    other = swap_seq(rows, 1)
    whole = jnp.where(
        core == 0, jnp.concatenate([rows, other], axis=1), jnp.concatenate([other, rows], axis=1)
    )
    return whole.astype(F32)


def vector_sum(flat, place, core):
    dp = lax.axis_size("dp")
    x, dp_index = place
    flat = flat + swap_seq(flat, 1)
    flat = flat + swap_seq(flat, 2)
    bits = dp.bit_length() - 1
    block = flat.reshape((2,) * bits + (flat.shape[1],))
    for bit in range(bits):
        axis = bits - 1 - bit
        mine = (dp_index >> bit) & 1
        sent = lax.dynamic_index_in_dim(block, 1 - mine, axis, keepdims=False)
        kept = lax.dynamic_index_in_dim(block, mine, axis, keepdims=False)
        block = kept + swap_dp(sent, 1 << bit)
    return block


def per_device(
    tokens, lengths, centre_flags, cotangent, mask_vector, qkv_weight, qv_bias, out_weight, out_bias,
    attn_gain, attn_shift, up_weight, up_bias, down_weight, down_bias, ffn_gain, ffn_shift,
):
    seq = lax.axis_index("seq")
    x, core = seq // 2, seq % 2
    place = (x, lax.axis_index("dp"))
    stretch = tokens.shape[1]

    def one_slot(array):
        own = lax.dynamic_index_in_dim(array, x, 0, keepdims=False)
        other = lax.dynamic_index_in_dim(array, 1 - x, 0, keepdims=False)
        return jnp.concatenate([own, swap_seq(other, 2)], axis=0)

    def two_slots(own, other):
        return jnp.where(x == 0, jnp.stack([own, other]), jnp.stack([other, own]))

    flags = one_slot(centre_flags).reshape(2, stretch)
    flags_peer = swap_seq(flags, 1)
    by_offset = jnp.stack([flags[0], flags_peer[0], flags[1], flags_peer[1]])
    ordered = jnp.take(by_offset, jnp.arange(4) ^ seq, axis=0).reshape(-1)
    length = ordered.shape[0]
    padded = jnp.pad(ordered, (SPAN, SPAN))
    count = padded[0:length]
    for offset in range(1, 2 * SPAN + 1):
        count = count + padded[offset : offset + length]
    masked_all = (count > 0).astype(F32).reshape(4, stretch)
    masked = jnp.take(masked_all, jnp.stack([seq, seq ^ 2]), axis=0).reshape(-1, 1)

    slot_length = lax.dynamic_index_in_dim(lengths, x, 0, keepdims=False)
    offsets = jnp.arange(stretch, dtype=jnp.int32)
    positions = jnp.concatenate([offsets + stretch * (seq ^ k) for k in (0, 2, 1, 3)])
    keep = positions < slot_length

    hidden = one_slot(tokens).astype(F32) * (1.0 - masked) + masked * mask_vector
    all_params = (
        qkv_weight, qv_bias, out_weight, out_bias, attn_gain, attn_shift,
        up_weight, up_bias, down_weight, down_bias, ffn_gain, ffn_shift,
    )
    layers = qkv_weight.shape[0]
    saved_states = []
    for layer in range(layers):
        hidden, saved = layer_forward(hidden, tuple(weight[layer] for weight in all_params), keep)
        saved_states.append(saved)
    layer_out = two_slots(hidden[:stretch], swap_seq(hidden[stretch:], 2))

    upstream = one_slot(cotangent).astype(F32)
    shares, vectors = [None] * layers, [None] * layers
    for layer in reversed(range(layers)):
        upstream, matrices, vectors[layer] = layer_backward(
            upstream, tuple(weight[layer] for weight in all_params), saved_states[layer], keep, core
        )
        firsts = (True, False, True, False) if layer % 2 else (False, True, False, True)
        shares[layer] = [scatter_sum(m, place, f) for m, f in zip(matrices, firsts)]
    input_grad = upstream * (1.0 - masked)
    input_grad = two_slots(input_grad[:stretch], swap_seq(input_grad[stretch:].astype(BF16), 2).astype(F32))
    mask_term = jnp.sum(upstream * masked, axis=0)

    dp = lax.axis_size("dp")
    parts = [v.reshape(dp, -1) for terms in vectors for v in terms] + [mask_term.reshape(dp, -1)]
    summed = vector_sum(jnp.concatenate(parts, axis=1), place, core)
    cuts, at = [], 0
    for part in parts:
        cuts.append(summed[at : at + part.shape[1]])
        at += part.shape[1]
    per_layer = len(vectors[0])
    stacked = [jnp.stack([cuts[layer * per_layer + i] for layer in range(layers)]) for i in range(per_layer)]
    qkv_grad, out_grad, up_grad, down_grad = (
        jnp.stack([gather_share(shares[layer][i], x, core) for layer in range(layers)]) for i in range(4)
    )
    return (
        layer_out, input_grad, cuts[-1], qkv_grad, stacked[0], out_grad, stacked[1], stacked[2], stacked[3],
        up_grad, stacked[4], down_grad, stacked[5], stacked[6], stacked[7],
    )


def solution(mesh):
    rows = P("dp", "seq", None)
    placed = (rows, P("dp"), P("dp", "seq"), rows) + (P(),) * 13
    matrix, vector = P(None, "dp", None), P(None, "dp")
    return jax.shard_map(
        per_device,
        mesh=mesh,
        in_specs=placed,
        out_specs=(
            rows, rows, P("dp"), matrix, vector, matrix, vector, vector, vector,
            matrix, vector, matrix, vector, vector, vector,
        ),
        check_vma=False,
    )
```

time: 1940 us -> 430 us (0.22)
  waiting for transfers between devices: 1670 us -> 149 us
  starting transfers between devices: 5.69 us -> 71.3 us
  other arithmetic: 74.5 us -> 52 us
    reduce_scatter x8 -> x0, waiting for transfers between devices: 970 us -> none  [the longest x1 314 us: per_device(): lax.psum_scatter(stacked[6], 'dp', scatter_dimension=1, tiled=True)]
    unnamed x31 -> x0, waiting for transfers between devices: 569 us -> none
    ppermute x2 -> x83, waiting for transfers between devices: 0.11 us -> 149 us  [the longest x27 87 us: swap_dp(): return lax.ppermute(value, 'dp', [(i, i ^ bit) for i in range(count)])]
    ppermute x2 -> x83, starting transfers between devices: 4.31 us -> 71.3 us  [the longest x27 37.9 us: swap_dp(): return lax.ppermute(value, 'dp', [(i, i ^ bit) for i in range(count)])]
    psum x1 -> x0, waiting for transfers between devices: 65.9 us -> none  [per_device(): lax.psum(shares[0].astype(jnp.bfloat16), 'seq').astype(jnp.float32)]
    all_gather x4 -> x0, waiting for transfers between devices: 65.4 us -> none  [the longest x2 36.3 us: layer_forward(): lax.all_gather(key_local, 'seq', axis=1, tiled=True)]
    unnamed x305 -> x280, local copies, waits for them, and re-layouts: 33 us -> 8.61 us
  transfers between devices with their start and end apart: 24 -> 83, of which waited for: 22 -> 33; matrix products, arithmetic and copies ran while one was open for 7% -> 39% of each run, Pallas kernels for 0% -> 0%
where the time goes in v1:
time: 430 us; the launch traced here: 425 us
  waiting for transfers between devices  149 us (35%)
  matrix products  85.4 us (20%)
  starting transfers between devices  71.3 us (17%)
  local copies, waits for them, and re-layouts  64.1 us (15%)
  other arithmetic  52 us (12%)
    ppermute x27, waiting for transfers between devices, swap_dp(): return lax.ppermute(value, 'dp', [(i, i ^ bit) for i in range(count)])  87 us
    ppermute x56, waiting for transfers between devices, swap_seq(): return lax.ppermute(value, 'seq', [(i, i ^ bit) for i in range(count)])  61.6 us
    ppermute x27, starting transfers between devices, swap_dp(): return lax.ppermute(value, 'dp', [(i, i ^ bit) for i in range(count)])  37.9 us
    ppermute x56, starting transfers between devices, swap_seq(): return lax.ppermute(value, 'seq', [(i, i ^ bit) for i in range(count)])  33.5 us
    dot_general x8, matrix products, dot_bt(): lax.dot_general(a, b, (((1,), (1,)), ((), ())), preferred_element_type=F32)  22.3 us
    dot_general x8, matrix products, dot(): lax.dot_general(a, b, (((1,), (0,)), ((), ())), preferred_element_type=F32)  19 us
    dot_general x8, matrix products, dot_at(): lax.dot_general(a, b, (((0,), (0,)), ((), ())), preferred_element_type=F32)  17.7 us
    reshape x14, local copies, waits for them, and re-layouts, per_device(): v.reshape(dp, -1)  12.1 us
  transfers between devices with their start and end apart: 83, of which 33 were waited for; matrix products, arithmetic and copies ran while one was open for 39% of the time, Pallas kernels for 0%

profile of v1, /device:TPU:0, one launch (start us, length us, event | category | flops | bytes accessed | tf_op | source)
XLA Modules:
  0.0 425.1 jit_solution(6198100797474911041)
XLA Ops:
  1.4 2.9 collective-permute-start.1
  15.5 3.2 fusion.52
  30.0 2.8 fusion.125
  35.9 3.1 multiply_convert_fusion.3
  59.6 2.9 fusion.124
  65.5 2.6 multiply_convert_fusion.2
  76.0 3.0 multiply_reduce_fusion.3
  83.4 4.0 fusion.90
  108.1 4.1 multiply_reduce_fusion.4
  113.2 4.6 %convert_reduce_fusion.1 = (f32[3072]{0:T(1024)}, bf16[256,3072]{1,0:T(8,128)(2,1)S(1)}) fusion(f32[256,3072]{1,0:T(8,128)S(1)} %copy-done.117, bf16[256,768]{1,0:T(8,128)(2,1)S(1)} %get-tuple-element.57, bf16[2,3072,768]{2,1,0:T(8,128)(2,1)} %param.30), kind=kOutput, calls=%fused_computation.79 | convolution fusion | flops 1217393664 | bytes 9842688 | tf_op jit(solution)/shard_map/dot_general | solution.py:64
  123.3 5.2 %fusion.93 = f32[512,12,64]{0,2,1:T(8,128)} fusion(bf16[256,12,64]{0,2,1:T(8,128)(2,1)S(1)} %bitcast.514, f32[12,256,512]{2,1,0:T(8,128)} %copy-done, f32[12,256]{1,0:T(8,128)S(1)} %log_add_fusion), kind=kOutput, calls=%fused_computation.113 | convolution fusion | flops 204472320 | bytes 8269824 | tf_op jit(solution)/shard_map/hqk,qhe->khe/dot_general | solution.py:94
  176.0 4.2 multiply_reduce_fusion.2
  192.2 2.9 collective-permute-done.15
  200.3 3.6 collective-permute-done.16
  210.0 2.7 convolution_convert_fusion.4
  212.9 2.7 collective-permute-done.13
  219.5 2.7 collective-permute-start.18
  235.1 2.6 collective-permute-start.40
  242.1 2.6 convolution_convert_fusion.3
  260.3 37.3 %collective-permute-done.29 = bf16[2,2,2,48,1152]{4,3,0,1,2:T(8,128)(2,1)S(1)} collective-permute-done((bf16[2,2,2,48,1152]{4,3,0,1,2:T(8,128)(2,1)S(1)}, bf16[2,2,2,48,1152]{4,3,0,1,2:T(8,128)(2,1)S(1)}, u32[]{:S(2)}, u32[]{:S(2)}) %collective-permute-start.29) | collective-permute-done | bytes 884768 | tf_op jit(solution)/shard_map/ppermute | solution.py:22
  300.3 3.5 collective-permute-done.21
  305.6 33.0 %collective-permute-done.30 = bf16[2,2,48,1152]{3,2,0,1:T(8,128)(2,1)S(1)} collective-permute-done((bf16[2,2,48,1152]{3,2,0,1:T(8,128)(2,1)S(1)}, bf16[2,2,48,1152]{3,2,0,1:T(8,128)(2,1)S(1)}, u32[]{:S(2)}, u32[]{:S(2)}) %collective-permute-start.30) | collective-permute-done | bytes 442400 | tf_op jit(solution)/shard_map/ppermute | solution.py:27
  346.9 4.4 %collective-permute-done.62 = bf16[2,2,48,1536]{3,2,0,1:T(8,128)(2,1)S(1)} collective-permute-done((bf16[2,2,48,1536]{3,2,0,1:T(8,128)(2,1)S(1)}, bf16[2,2,48,1536]{3,2,0,1:T(8,128)(2,1)S(1)}, u32[]{:S(2)}, u32[]{:S(2)}) %collective-permute-start.62) | collective-permute-done | bytes 589856 | tf_op jit(solution)/shard_map/ppermute | solution.py:27
  351.3 2.6 collective-permute-start.32
  354.1 4.1 collective-permute-done.32
  362.4 2.6 collective-permute-done.33
  373.8 6.5 %collective-permute-done.64 = bf16[48,1536]{1,0:T(8,128)(2,1)S(1)} collective-permute-done((bf16[48,1536]{1,0:T(8,128)(2,1)S(1)}, bf16[48,1536]{1,0:T(8,128)(2,1)S(1)}, u32[]{:S(2)}, u32[]{:S(2)}) %collective-permute-start.64) | collective-permute-done | bytes 147488 | tf_op jit(solution)/shard_map/ppermute | solution.py:27
  383.6 2.9 collective-permute-done.65
  395.2 7.4 %collective-permute-done.72 = bf16[192,384]{1,0:T(8,128)(2,1)S(1)} collective-permute-done((bf16[192,384]{1,0:T(8,128)(2,1)S(1)}, bf16[192,384]{1,0:T(8,128)(2,1)S(1)}, u32[]{:S(2)}, u32[]{:S(2)}) %collective-permute-start.72) | collective-permute-done | bytes 147488 | tf_op jit(solution)/shard_map/ppermute | solution.py:27
  408.4 2.7 collective-permute-done.57
  411.9 4.2 collective-permute-done.80
  417.7 3.7 collective-permute-done.81
  (703 shorter events, 243.7 us)
Async XLA Ops:
  46.6 23.4 %collective-permute-start.8 = (bf16[128,768]{1,0:T(8,128)(2,1)}, bf16[128,768]{1,0:T(8,128)(2,1)}, u32[]{:S(2)}, u32[]{:S(2)}) collective-permute-start(bf16[128,768]{1,0:T(8,128)(2,1)} %get-tuple-element.108), channel_id=1, source_target_pairs={{0,2},{1,3},{2,0},{3,1},{4,6},{5,7},{6,4},{7,5},{8,10},{9,11},{10,... | collective-permute-start | bytes 589832 | tf_op jit(solution)/shard_map/ppermute | solution.py:22
  48.6 202.7 %collective-permute-start.19 = (bf16[256,768]{1,0:T(8,128)(2,1)}, bf16[256,768]{1,0:T(8,128)(2,1)}, u32[]{:S(2)}, u32[]{:S(2)}) collective-permute-start(bf16[256,768]{1,0:T(8,128)(2,1)} %fusion.179), channel_id=1, source_target_pairs={{0,1},{1,0},{2,3},{3,2},{4,5},{5,4},{6,7},{7,6},{8,9},{9,8},{10,11... | collective-permute-start | bytes 1179656 | tf_op jit(solution)/shard_map/ppermute | solution.py:22
  48.7 111.2 %collective-permute-start.35 = (bf16[256,768]{0,1:T(8,128)(2,1)}, bf16[256,768]{0,1:T(8,128)(2,1)}, u32[]{:S(2)}, u32[]{:S(2)}) collective-permute-start(bf16[256,768]{0,1:T(8,128)(2,1)} %bitcast.26), channel_id=1, source_target_pairs={{0,1},{1,0},{2,3},{3,2},{4,5},{5,4},{6,7},{7,6},{8,9},{9,8},{10,11... | collective-permute-start | bytes 1179656 | tf_op jit(solution)/shard_map/ppermute | solution.py:22
  62.4 74.3 %collective-permute-start.43 = (bf16[256,768]{0,1:T(8,128)(2,1)}, bf16[256,768]{0,1:T(8,128)(2,1)}, u32[]{:S(2)}, u32[]{:S(2)}) collective-permute-start(bf16[256,768]{0,1:T(8,128)(2,1)} %bitcast.36), channel_id=1, source_target_pairs={{0,1},{1,0},{2,3},{3,2},{4,5},{5,4},{6,7},{7,6},{8,9},{9,8},{10,11... | collective-permute-start | bytes 1179656 | tf_op jit(solution)/shard_map/ppermute | solution.py:22
  104.9 31.9 %collective-permute-start.44 = (bf16[256,384]{1,0:T(8,128)(2,1)}, bf16[256,384]{1,0:T(8,128)(2,1)}, u32[]{:S(2)}, u32[]{:S(2)}) collective-permute-start(bf16[256,384]{1,0:T(8,128)(2,1)} %get-tuple-element.106), channel_id=1, source_target_pairs={{0,1},{1,0},{2,3},{3,2},{4,5},{5,4},{6,7},{7,6},{8,9},{9,8},{10,11... | collective-permute-start | bytes 589832 | tf_op jit(solution)/shard_map/ppermute | solution.py:22
  106.8 33.5 %collective-permute-start.7 = (f32[128,768]{1,0:T(8,128)}, f32[128,768]{1,0:T(8,128)}, u32[]{:S(2)}, u32[]{:S(2)}) collective-permute-start(f32[128,768]{1,0:T(8,128)} %get-tuple-element.94), channel_id=1, source_target_pairs={{0,2},{1,3},{2,0},{3,1},{4,6},{5,7},{6,4},{7,5},{8,10},{9,11},{10,... | collective-permute-start | bytes 1179656 | tf_op jit(solution)/shard_map/ppermute | solution.py:22
  136.8 29.3 %collective-permute-start.60 = (bf16[256,1536]{1,0:T(8,128)(2,1)}, bf16[256,1536]{1,0:T(8,128)(2,1)}, u32[]{:S(2)}, u32[]{:S(2)}) collective-permute-start(bf16[256,1536]{1,0:T(8,128)(2,1)} %get-tuple-element.85), channel_id=1, source_target_pairs={{0,1},{1,0},{2,3},{3,2},{4,5},{5,4},{6,7},{7,6},{8,9},{9,8},{10,11... | collective-permute-start | bytes 2359304 | tf_op jit(solution)/shard_map/ppermute | solution.py:22
  144.1 19.6 %collective-permute-start.45 = (bf16[2,2,2,48,384]{4,3,0,1,2:T(8,128)(2,1)}, bf16[2,2,2,48,384]{4,3,0,1,2:T(8,128)(2,1)}, u32[]{:S(2)}, u32[]{:S(2)}) collective-permute-start(bf16[2,2,2,48,384]{4,3,0,1,2:T(8,128)(2,1)} %bitcast.500), channel_id=1, source_target_pairs={{0,4},{4,0},{8,12},{12,8},{16,20},{20,16},{24,28},{28,24},{1,5},{5... | collective-permute-start | bytes 884744 | tf_op jit(solution)/shard_map/ppermute | solution.py:27
  159.8 80.2 %collective-permute-start.51 = (bf16[256,768]{1,0:T(8,128)(2,1)}, bf16[256,768]{1,0:T(8,128)(2,1)}, u32[]{:S(2)}, u32[]{:S(2)}) collective-permute-start(bf16[256,768]{1,0:T(8,128)(2,1)} %copy-done.53), channel_id=1, source_target_pairs={{0,1},{1,0},{2,3},{3,2},{4,5},{5,4},{6,7},{7,6},{8,9},{9,8},{10,11... | collective-permute-start | bytes 1179656 | tf_op jit(solution)/shard_map/ppermute | solution.py:22
  163.8 44.1 %collective-permute-start.27 = (bf16[256,768]{1,0:T(8,128)(2,1)}, bf16[256,768]{1,0:T(8,128)(2,1)}, u32[]{:S(2)}, u32[]{:S(2)}) collective-permute-start(bf16[256,768]{1,0:T(8,128)(2,1)} %fusion.181), channel_id=1, source_target_pairs={{0,1},{1,0},{2,3},{3,2},{4,5},{5,4},{6,7},{7,6},{8,9},{9,8},{10,11... | collective-permute-start | bytes 1179656 | tf_op jit(solution)/shard_map/ppermute | solution.py:22
  170.2 16.0 %collective-permute-start.37 = (bf16[2,2,2,48,384]{4,3,0,1,2:T(8,128)(2,1)}, bf16[2,2,2,48,384]{4,3,0,1,2:T(8,128)(2,1)}, u32[]{:S(2)}, u32[]{:S(2)}) collective-permute-start(bf16[2,2,2,48,384]{4,3,0,1,2:T(8,128)(2,1)} %bitcast.501), channel_id=1, source_target_pairs={{0,2},{1,3},{2,0},{3,1},{4,6},{5,7},{6,4},{7,5},{8,10},{9,11},{10,... | collective-permute-start | bytes 884744 | tf_op jit(solution)/shard_map/ppermute | solution.py:22
  185.9 22.6 %collective-permute-start.28 = (bf16[256,1152]{0,1:T(8,128)(2,1)}, bf16[256,1152]{0,1:T(8,128)(2,1)}, u32[]{:S(2)}, u32[]{:S(2)}) collective-permute-start(bf16[256,1152]{0,1:T(8,128)(2,1)} %get-tuple-element.89), channel_id=1, source_target_pairs={{0,1},{1,0},{2,3},{3,2},{4,5},{5,4},{6,7},{7,6},{8,9},{9,8},{10,11... | collective-permute-start | bytes 1769480 | tf_op jit(solution)/shard_map/ppermute | solution.py:22
  207.9 38.4 %collective-permute-start.67 = (bf16[256,3072]{1,0:T(8,128)(2,1)}, bf16[256,3072]{1,0:T(8,128)(2,1)S(1)}, u32[]{:S(2)}, u32[]{:S(2)}) collective-permute-start(bf16[256,3072]{1,0:T(8,128)(2,1)} %copy-done.112), channel_id=1, source_target_pairs={{0,1},{1,0},{2,3},{3,2},{4,5},{5,4},{6,7},{7,6},{8,9},{9,8},{10,11... | collective-permute-start | bytes 4718600 | tf_op jit(solution)/shard_map/ppermute | solution.py:22
  207.9 32.6 %collective-permute-start.52 = (bf16[256,1536]{1,0:T(8,128)(2,1)S(1)}, bf16[256,1536]{1,0:T(8,128)(2,1)S(1)}, u32[]{:S(2)}, u32[]{:S(2)}) collective-permute-start(bf16[256,1536]{1,0:T(8,128)(2,1)S(1)} %copy-done.46), channel_id=1, source_target_pairs={{0,1},{1,0},{2,3},{3,2},{4,5},{5,4},{6,7},{7,6},{8,9},{9,8},{10,11... | collective-permute-start | bytes 2359304 | tf_op jit(solution)/shard_map/ppermute | solution.py:22
  240.0 17.6 %collective-permute-start.75 = (bf16[256,3072]{1,0:T(8,128)(2,1)S(1)}, bf16[256,3072]{1,0:T(8,128)(2,1)S(1)}, u32[]{:S(2)}, u32[]{:S(2)}) collective-permute-start(bf16[256,3072]{1,0:T(8,128)(2,1)S(1)} %copy-done.115), channel_id=1, source_target_pairs={{0,1},{1,0},{2,3},{3,2},{4,5},{5,4},{6,7},{7,6},{8,9},{9,8},{10,11... | collective-permute-start | bytes 4718600 | tf_op jit(solution)/shard_map/ppermute | solution.py:22
  249.9 49.5 %collective-permute-start.61 = (bf16[2,2,2,48,1536]{4,3,0,1,2:T(8,128)(2,1)S(1)}, bf16[2,2,2,48,1536]{4,3,0,1,2:T(8,128)(2,1)S(1)}, u32[]{:S(2)}, u32[]{:S(2)}) collective-permute-start(bf16[2,2,2,48,1536]{4,3,0,1,2:T(8,128)(2,1)S(1)} %bitcast.534), channel_id=1, source_target_pairs={{0,2},{1,3},{2,0},{3,1},{4,6},{5,7},{6,4},{7,5},{8,10},{9,11},{10,... | collective-permute-start | bytes 3538952 | tf_op jit(solution)/shard_map/ppermute | solution.py:22
  251.3 46.3 %collective-permute-start.29 = (bf16[2,2,2,48,1152]{4,3,0,1,2:T(8,128)(2,1)S(1)}, bf16[2,2,2,48,1152]{4,3,0,1,2:T(8,128)(2,1)S(1)}, u32[]{:S(2)}, u32[]{:S(2)}) collective-permute-start(bf16[2,2,2,48,1152]{4,3,0,1,2:T(8,128)(2,1)S(1)} %bitcast.542), channel_id=1, source_target_pairs={{0,2},{1,3},{2,0},{3,1},{4,6},{5,7},{6,4},{7,5},{8,10},{9,11},{10,... | collective-permute-start | bytes 2654216 | tf_op jit(solution)/shard_map/ppermute | solution.py:22
  252.8 87.5 %collective-permute-start.69 = (bf16[2,2,2,192,384]{4,3,0,1,2:T(8,128)(2,1)S(1)}, bf16[2,2,2,192,384]{4,3,0,1,2:T(8,128)(2,1)S(1)}, u32[]{:S(2)}, u32[]{:S(2)}) collective-permute-start(bf16[2,2,2,192,384]{4,3,0,1,2:T(8,128)(2,1)S(1)} %bitcast.537), channel_id=1, source_target_pairs={{0,2},{1,3},{2,0},{3,1},{4,6},{5,7},{6,4},{7,5},{8,10},{9,11},{10,... | collective-permute-start | bytes 3538952 | tf_op jit(solution)/shard_map/ppermute | solution.py:22
  255.9 86.4 %collective-permute-start.53 = (bf16[2,2,2,48,1536]{4,3,0,1,2:T(8,128)(2,1)S(1)}, bf16[2,2,2,48,1536]{4,3,0,1,2:T(8,128)(2,1)S(1)}, u32[]{:S(2)}, u32[]{:S(2)}) collective-permute-start(bf16[2,2,2,48,1536]{4,3,0,1,2:T(8,128)(2,1)S(1)} %bitcast.535), channel_id=1, source_target_pairs={{0,4},{4,0},{8,12},{12,8},{16,20},{20,16},{24,28},{28,24},{1,5},{5... | collective-permute-start | bytes 3538952 | tf_op jit(solution)/shard_map/ppermute | solution.py:27
  257.5 46.3 %collective-permute-start.21 = (bf16[2,2,2,48,1152]{4,3,0,1,2:T(8,128)(2,1)S(1)}, bf16[2,2,2,48,1152]{4,3,0,1,2:T(8,128)(2,1)S(1)}, u32[]{:S(2)}, u32[]{:S(2)}) collective-permute-start(bf16[2,2,2,48,1152]{4,3,0,1,2:T(8,128)(2,1)S(1)} %bitcast.543), channel_id=1, source_target_pairs={{0,4},{4,0},{8,12},{12,8},{16,20},{20,16},{24,28},{28,24},{1,5},{5... | collective-permute-start | bytes 2654216 | tf_op jit(solution)/shard_map/ppermute | solution.py:27
  297.6 63.1 %collective-permute-start.77 = (bf16[2,2,2,192,384]{4,3,0,1,2:T(8,128)(2,1)S(1)}, bf16[2,2,2,192,384]{4,3,0,1,2:T(8,128)(2,1)S(1)}, u32[]{:S(2)}, u32[]{:S(2)}) collective-permute-start(bf16[2,2,2,192,384]{4,3,0,1,2:T(8,128)(2,1)S(1)} %bitcast.536), channel_id=1, source_target_pairs={{0,4},{4,0},{8,12},{12,8},{16,20},{20,16},{24,28},{28,24},{1,5},{5... | collective-permute-start | bytes 3538952 | tf_op jit(solution)/shard_map/ppermute | solution.py:27
  299.4 39.2 %collective-permute-start.30 = (bf16[2,2,48,1152]{3,2,0,1:T(8,128)(2,1)S(1)}, bf16[2,2,48,1152]{3,2,0,1:T(8,128)(2,1)S(1)}, u32[]{:S(2)}, u32[]{:S(2)}) collective-permute-start(bf16[2,2,48,1152]{3,2,0,1:T(8,128)(2,1)S(1)} %dynamic-slice_bitcast_fusion.4), channel_id=1, source_target_pairs={{0,4},{4,0},{8,12},{12,8},{16,20},{20,16},{24,28},{28,24},{1,5},{5... | collective-permute-start | bytes 1327112 | tf_op jit(solution)/shard_map/ppermute | solution.py:27
  303.9 47.4 %collective-permute-start.62 = (bf16[2,2,48,1536]{3,2,0,1:T(8,128)(2,1)S(1)}, bf16[2,2,48,1536]{3,2,0,1:T(8,128)(2,1)S(1)}, u32[]{:S(2)}, u32[]{:S(2)}) collective-permute-start(bf16[2,2,48,1536]{3,2,0,1:T(8,128)(2,1)S(1)} %dynamic-slice_bitcast_fusion.2), channel_id=1, source_target_pairs={{0,4},{4,0},{8,12},{12,8},{16,20},{20,16},{24,28},{28,24},{1,5},{5... | collective-permute-start | bytes 1769480 | tf_op jit(solution)/shard_map/ppermute | solution.py:27
  338.6 20.4 %collective-permute-start.22 = (bf16[2,2,48,1152]{3,2,0,1:T(8,128)(2,1)S(1)}, bf16[2,2,48,1152]{3,2,0,1:T(8,128)(2,1)S(1)}, u32[]{:S(2)}, u32[]{:S(2)}) collective-permute-start(bf16[2,2,48,1152]{3,2,0,1:T(8,128)(2,1)S(1)} %dynamic-slice_bitcast_fusion.5), channel_id=1, source_target_pairs={{0,2},{1,3},{2,0},{3,1},{4,6},{5,7},{6,4},{7,5},{8,10},{9,11},{10,... | collective-permute-start | bytes 1327112 | tf_op jit(solution)/shard_map/ppermute | solution.py:22
  342.3 28.0 %collective-permute-start.70 = (bf16[2,2,192,384]{3,2,0,1:T(8,128)(2,1)S(1)}, bf16[2,2,192,384]{3,2,0,1:T(8,128)(2,1)S(1)}, u32[]{:S(2)}, u32[]{:S(2)}) collective-permute-start(bf16[2,2,192,384]{3,2,0,1:T(8,128)(2,1)S(1)} %dynamic-slice_bitcast_fusion.1), channel_id=1, source_target_pairs={{0,4},{4,0},{8,12},{12,8},{16,20},{20,16},{24,28},{28,24},{1,5},{5... | collective-permute-start | bytes 1769480 | tf_op jit(solution)/shard_map/ppermute | solution.py:27
  346.3 25.0 %collective-permute-start.54 = (bf16[2,2,48,1536]{3,2,0,1:T(8,128)(2,1)S(1)}, bf16[2,2,48,1536]{3,2,0,1:T(8,128)(2,1)S(1)}, u32[]{:S(2)}, u32[]{:S(2)}) collective-permute-start(bf16[2,2,48,1536]{3,2,0,1:T(8,128)(2,1)S(1)} %dynamic-slice_bitcast_fusion.3), channel_id=1, source_target_pairs={{0,2},{1,3},{2,0},{3,1},{4,6},{5,7},{6,4},{7,5},{8,10},{9,11},{10,... | collective-permute-start | bytes 1769480 | tf_op jit(solution)/shard_map/ppermute | solution.py:22
  365.0 26.8 %collective-permute-start.78 = (bf16[2,2,192,384]{3,2,0,1:T(8,128)(2,1)S(1)}, bf16[2,2,192,384]{3,2,0,1:T(8,128)(2,1)S(1)}, u32[]{:S(2)}, u32[]{:S(2)}) collective-permute-start(bf16[2,2,192,384]{3,2,0,1:T(8,128)(2,1)S(1)} %dynamic-slice_bitcast_fusion), channel_id=1, source_target_pairs={{0,2},{1,3},{2,0},{3,1},{4,6},{5,7},{6,4},{7,5},{8,10},{9,11},{10,... | collective-permute-start | bytes 1769480 | tf_op jit(solution)/shard_map/ppermute | solution.py:22
  371.3 17.3 %collective-permute-start.71 = (bf16[2,192,384]{2,1,0:T(8,128)(2,1)S(1)}, bf16[2,192,384]{2,1,0:T(8,128)(2,1)S(1)}, u32[]{:S(2)}, u32[]{:S(2)}) collective-permute-start(bf16[2,192,384]{2,1,0:T(8,128)(2,1)S(1)} %dynamic-slice_bitcast_fusion.7), channel_id=1, source_target_pairs={{0,8},{4,12},{8,0},{12,4},{16,24},{20,28},{24,16},{28,20},{1,9},{5... | collective-permute-start | bytes 884744 | tf_op jit(solution)/shard_map/ppermute | solution.py:27
  373.3 17.9 %collective-permute-start.55 = (bf16[2,48,1536]{2,1,0:T(8,128)(2,1)S(1)}, bf16[2,48,1536]{2,1,0:T(8,128)(2,1)S(1)}, u32[]{:S(2)}, u32[]{:S(2)}) collective-permute-start(bf16[2,48,1536]{2,1,0:T(8,128)(2,1)S(1)} %dynamic-slice_bitcast_fusion.9), channel_id=1, source_target_pairs={{0,8},{4,12},{8,0},{12,4},{16,24},{20,28},{24,16},{28,20},{1,9},{5... | collective-permute-start | bytes 884744 | tf_op jit(solution)/shard_map/ppermute | solution.py:27
  386.6 19.9 %collective-permute-start.66 = (bf16[96,1536]{1,0:T(8,128)(2,1)S(1)}, bf16[96,1536]{1,0:T(8,128)(2,1)S(1)}, u32[]{:S(2)}, u32[]{:S(2)}) collective-permute-start(bf16[96,1536]{1,0:T(8,128)(2,1)S(1)} %maximum_select_fusion.9), channel_id=1, source_target_pairs={{0,1},{1,0},{2,3},{3,2},{4,5},{5,4},{6,7},{7,6},{8,9},{9,8},{10,11... | collective-permute-start | bytes 884744 | tf_op jit(solution)/shard_map/ppermute | solution.py:22
  391.3 14.1 %collective-permute-start.56 = (bf16[48,1536]{1,0:T(8,128)(2,1)S(1)}, bf16[48,1536]{1,0:T(8,128)(2,1)S(1)}, u32[]{:S(2)}, u32[]{:S(2)}) collective-permute-start(bf16[48,1536]{1,0:T(8,128)(2,1)S(1)} %dynamic-slice_bitcast_fusion.19), channel_id=1, source_target_pairs={{0,16},{4,20},{8,24},{12,28},{16,0},{20,4},{24,8},{28,12},{1,17},{... | collective-permute-start | bytes 442376 | tf_op jit(solution)/shard_map/ppermute | solution.py:27
  392.1 14.8 %collective-permute-start.79 = (bf16[2,192,384]{2,1,0:T(8,128)(2,1)S(1)}, bf16[2,192,384]{2,1,0:T(8,128)(2,1)S(1)}, u32[]{:S(2)}, u32[]{:S(2)}) collective-permute-start(bf16[2,192,384]{2,1,0:T(8,128)(2,1)S(1)} %dynamic-slice_bitcast_fusion.6), channel_id=1, source_target_pairs={{0,8},{4,12},{8,0},{12,4},{16,24},{20,28},{24,16},{28,20},{1,9},{5... | collective-permute-start | bytes 884744 | tf_op jit(solution)/shard_map/ppermute | solution.py:27
  (193 other events, 1035.6 us)

commit v2 on v1

v2 whole, which is shorter than its diff:
```python
import functools
import math

import jax
import jax.numpy as jnp
from jax import lax
from jax.experimental import pallas as pl
from jax.experimental.pallas import tpu as pltpu
from jax.sharding import PartitionSpec as P

SPAN = 5
NEG_FILL = -1000000000.0
LN_EPS = 1e-12
ROOT_HALF = 0.7071067811865476
INV_ROOT_TAU = 0.3989422804014327
F32 = jnp.float32
BF16 = jnp.bfloat16
HEAD = 64
PAIR = 128


def dot(a, b):
    return lax.dot_general(a, b, (((1,), (0,)), ((), ())), preferred_element_type=F32)


def dot_bt(a, b):
    return lax.dot_general(a, b, (((1,), (1,)), ((), ())), preferred_element_type=F32)


def dot_at(a, b):
    return lax.dot_general(a, b, (((0,), (0,)), ((), ())), preferred_element_type=F32)


def total(values):
    return jnp.sum(values, axis=0, keepdims=True)


def mean(values):
    return jnp.mean(values, axis=-1, keepdims=True)


def norm_forward(summed):
    centred = summed - mean(summed)
    inverse = lax.rsqrt(mean(centred * centred) + LN_EPS)
    return centred * inverse, inverse


def norm_backward(upstream, unit, inverse, gain):
    pushed = upstream * gain
    return (pushed - mean(pushed) - unit * mean(pushed * unit)) * inverse


def gelu_pair(inputs):
    half = 0.5 + 0.5 * lax.erf(inputs * ROOT_HALF)
    return inputs * half, half + inputs * INV_ROOT_TAU * jnp.exp(-0.5 * inputs * inputs)


def head_masks(scale):
    lane = lax.broadcasted_iota(jnp.int32, (1, PAIR), 1)
    return [jnp.where((lane < HEAD) == (h == 0), scale, 0.0).astype(BF16) for h in range(2)]


def join_heads(parts):
    row = lax.broadcasted_iota(jnp.int32, parts[0].shape, 0)
    return jnp.where(row < HEAD, parts[0], parts[1]).T


def attention_forward(q_ref, own_ref, peer_ref, keep_ref, probs_ref, context_ref):
    width = q_ref.shape[1]
    scaled = head_masks(HEAD**-0.5)
    keep = keep_ref[...] > 0

    @pl.loop(0, width // PAIR)
    def _(j):
        at = pl.ds(pl.multiple_of(j * PAIR, PAIR), PAIR)
        at_v = pl.ds(pl.multiple_of(width + j * PAIR, PAIR), PAIR)
        q = q_ref[:, at]
        k = jnp.concatenate([own_ref[:, at], peer_ref[:, at]], axis=0)
        v = jnp.concatenate([own_ref[:, at_v], peer_ref[:, at_v]], axis=0)
        parts = []
        for h in range(2):
            scores = jnp.where(keep, dot_bt(k, q * scaled[h]), NEG_FILL)
            powers = jnp.exp(scores - jnp.max(scores, axis=0, keepdims=True))
            probs = (powers * (1.0 / total(powers))).astype(BF16)
            probs_ref[2 * j + h] = probs
            parts.append(dot_at(v, probs))
        context_ref[:, at] = join_heads(parts).astype(BF16)


def attention_backward(q_ref, own_ref, peer_ref, probs_ref, grad_ref, dq_ref, own_out, peer_out):
    width = q_ref.shape[1]
    rows = q_ref.shape[0]
    scaled, plain = head_masks(HEAD**-0.5), head_masks(1.0)

    @pl.loop(0, width // PAIR)
    def _(j):
        at = pl.ds(pl.multiple_of(j * PAIR, PAIR), PAIR)
        at_v = pl.ds(pl.multiple_of(width + j * PAIR, PAIR), PAIR)
        q, g = q_ref[:, at], grad_ref[:, at]
        k = jnp.concatenate([own_ref[:, at], peer_ref[:, at]], axis=0)
        v = jnp.concatenate([own_ref[:, at_v], peer_ref[:, at_v]], axis=0)
        parts, dk, dv = [], 0.0, 0.0
        for h in range(2):
            grad = g * plain[h]
            low = probs_ref[2 * j + h]
            probs = low.astype(F32)
            dv = dv + dot(low, grad)
            prob_grad = dot_bt(v, grad)
            score_grad = (probs * (prob_grad - total(prob_grad * probs))).astype(BF16)
            dk = dk + dot(score_grad, q * scaled[h])
            parts.append(dot_at(k, score_grad))
        dq_ref[:, at] = (join_heads(parts) * HEAD**-0.5).astype(BF16)
        own_out[:, at], own_out[:, at_v] = dk[:rows], dv[:rows]
        peer_out[:, at], peer_out[:, at_v] = dk[rows:].astype(BF16), dv[rows:].astype(BF16)


def project(low, weight_ref, bias, q_ref, kv_ref):
    width = low.shape[1]
    q_ref[...] = (dot(low, weight_ref[:, :width]) + bias[:, :width]).astype(BF16)
    kv_ref[:, :width] = dot(low, weight_ref[:, width : 2 * width]).astype(BF16)
    kv_ref[:, width:] = (dot(low, weight_ref[:, 2 * width :]) + bias[:, width:]).astype(BF16)


def feed_forward(ffn_in, up_ref, up_bias, down_ref, act_ref, slope_ref):
    width = ffn_in.shape[1]
    out = 0.0
    for j in range(up_ref.shape[1] // width):
        at = slice(j * width, (j + 1) * width)
        act, slope = gelu_pair(dot(ffn_in, up_ref[:, at]) + up_bias[:, at])
        act = act.astype(BF16)
        act_ref[:, at] = act
        slope_ref[:, at] = slope.astype(slope_ref.dtype)
        out = out + dot(act, down_ref[at, :])
    return out


def feed_backward(down_low, up_ref, down_ref, slope_ref, up_low_ref, sums_ref, first_row):
    width = down_low.shape[1]
    out = 0.0
    for j in range(up_ref.shape[1] // width):
        at = slice(j * width, (j + 1) * width)
        low = (dot_bt(down_low, down_ref[at, :]) * slope_ref[:, at].astype(F32)).astype(BF16)
        up_low_ref[:, at] = low
        sums_ref[first_row + j : first_row + j + 1, :] = total(low.astype(F32))
        out = out + dot_bt(low, up_ref[:, at])
    return out


class Fetch:
    def __init__(self, layer, pairs, sems):
        self.copies = [
            pltpu.make_async_copy(src.at[layer], dst, sems.at[i]) for i, (src, dst) in enumerate(pairs)
        ]
        for copy in self.copies:
            copy.start()

    def wait(self, *which):
        for i in which:
            self.copies[i].wait()


def first_kernel(
    own_ref, recv_ref, masked_ref, vector_ref, bias_ref, weight_any,
    hidden_ref, low_ref, q_ref, kv_ref,
    weight_ref, sems,
):
    fetch = Fetch(0, [(weight_any, weight_ref)], sems)
    tokens = jnp.concatenate([own_ref[...], recv_ref[...]], axis=0).astype(F32)
    masked = masked_ref[...]
    hidden = tokens * (1.0 - masked) + masked * vector_ref[...]
    hidden_ref[...] = hidden
    low = hidden.astype(BF16)
    low_ref[...] = low
    fetch.wait(0)
    project(low, weight_ref, bias_ref[0:1, :], q_ref, kv_ref)


def attend_and_norm(
    layer, q_ref, own_ref, peer_ref, keep_ref, hidden_ref, out_ref, out_bias_ref, gain_ref, shift_ref,
    probs_ref, context_ref, unit_ref, inverse_ref, ffn_in_ref, out_ready,
):
    this = slice(layer, layer + 1)
    attention_forward(q_ref, own_ref, peer_ref, keep_ref, probs_ref, context_ref)
    out_ready()
    attended = dot(context_ref[...], out_ref[...]) + out_bias_ref[this, :]
    unit, inverse = norm_forward(hidden_ref[...] + attended)
    unit_ref[...], inverse_ref[...] = unit, inverse
    normed = unit * gain_ref[this, :] + shift_ref[this, :]
    ffn_in_ref[...] = normed.astype(BF16)
    return normed


def forward_kernel(
    layer,
    q_ref, own_ref, peer_ref, keep_ref, hidden_ref, out_bias_ref, attn_gain_ref, attn_shift_ref,
    up_bias_ref, down_bias_ref, ffn_gain_ref, ffn_shift_ref, qv_bias_ref, out_any, up_any, down_any, qkv_any,
    probs_ref, context_ref, unit_one_ref, inverse_one_ref, ffn_in_ref, act_ref, slope_ref,
    unit_two_ref, inverse_two_ref, next_ref, next_low_ref, next_q_ref, next_kv_ref,
    out_ref, up_ref, down_ref, qkv_ref, sems,
):
    this = slice(layer, layer + 1)
    fetch = Fetch(layer, [(out_any, out_ref), (up_any, up_ref), (down_any, down_ref)], sems)
    fetch_next = Fetch(layer + 1, [(qkv_any, qkv_ref)], sems.at[pl.ds(3, 1)])
    normed = attend_and_norm(
        layer, q_ref, own_ref, peer_ref, keep_ref, hidden_ref, out_ref, out_bias_ref, attn_gain_ref,
        attn_shift_ref, probs_ref, context_ref, unit_one_ref, inverse_one_ref, ffn_in_ref,
        lambda: fetch.wait(0),
    )
    fetch.wait(1, 2)
    down = feed_forward(ffn_in_ref[...], up_ref, up_bias_ref[this, :], down_ref, act_ref, slope_ref)
    unit, inverse = norm_forward(normed + (down + down_bias_ref[this, :]))
    unit_two_ref[...], inverse_two_ref[...] = unit, inverse
    hidden = unit * ffn_gain_ref[this, :] + ffn_shift_ref[this, :]
    next_ref[...] = hidden
    low = hidden.astype(BF16)
    next_low_ref[...] = low
    fetch_next.wait(0)
    project(low, qkv_ref, qv_bias_ref[layer + 1 : layer + 2, :], next_q_ref, next_kv_ref)


def ffn_step_back(
    layer, upstream, unit, inverse, ffn_gain_ref, up_ref, down_ref, slope_ref,
    down_low_ref, up_low_ref, grad_normed_ref, sums_ref,
):
    sums_ref[0:1, :] = total(upstream * unit)
    sums_ref[1:2, :] = total(upstream)
    grad = norm_backward(upstream, unit, inverse, ffn_gain_ref[layer : layer + 1, :])
    low = grad.astype(BF16)
    down_low_ref[...] = low
    sums_ref[2:3, :] = total(low.astype(F32))
    grad_normed_ref[...] = grad + feed_backward(low, up_ref, down_ref, slope_ref, up_low_ref, sums_ref, 3)


def turn_kernel(
    layer,
    q_ref, own_ref, peer_ref, keep_ref, hidden_ref, cot_own_ref, cot_recv_ref, out_bias_ref, attn_gain_ref,
    attn_shift_ref, up_bias_ref, down_bias_ref, ffn_gain_ref, ffn_shift_ref, out_any, up_any, down_any,
    probs_ref, context_ref, unit_one_ref, inverse_one_ref, ffn_in_ref, act_ref, final_ref,
    down_low_ref, up_low_ref, grad_normed_ref, sums_ref,
    out_ref, up_ref, down_ref, slope_ref, sems,
):
    this = slice(layer, layer + 1)
    fetch = Fetch(layer, [(out_any, out_ref), (up_any, up_ref), (down_any, down_ref)], sems)
    normed = attend_and_norm(
        layer, q_ref, own_ref, peer_ref, keep_ref, hidden_ref, out_ref, out_bias_ref, attn_gain_ref,
        attn_shift_ref, probs_ref, context_ref, unit_one_ref, inverse_one_ref, ffn_in_ref,
        lambda: fetch.wait(0),
    )
    fetch.wait(1, 2)
    down = feed_forward(ffn_in_ref[...], up_ref, up_bias_ref[this, :], down_ref, act_ref, slope_ref)
    unit, inverse = norm_forward(normed + (down + down_bias_ref[this, :]))
    final_ref[...] = unit * ffn_gain_ref[this, :] + ffn_shift_ref[this, :]
    upstream = jnp.concatenate([cot_own_ref[...], cot_recv_ref[...]], axis=0).astype(F32)
    ffn_step_back(
        layer, upstream, unit, inverse, ffn_gain_ref, up_ref, down_ref, slope_ref,
        down_low_ref, up_low_ref, grad_normed_ref, sums_ref,
    )


def attend_back_kernel(
    layer,
    grad_ref, unit_ref, inverse_ref, gain_ref, q_ref, own_ref, peer_ref, probs_ref, out_any,
    mid_ref, low_ref, dq_ref, own_out, peer_out, sums_ref,
    out_ref, context_grad_ref, sems,
):
    fetch = Fetch(layer, [(out_any, out_ref)], sems)
    upstream, unit = grad_ref[...], unit_ref[...]
    sums_ref[0:1, :] = total(upstream * unit)
    sums_ref[1:2, :] = total(upstream)
    grad = norm_backward(upstream, unit, inverse_ref[...], gain_ref[layer : layer + 1, :])
    mid_ref[...] = grad
    low = grad.astype(BF16)
    low_ref[...] = low
    sums_ref[2:3, :] = total(low.astype(F32))
    fetch.wait(0)
    context_grad_ref[...] = dot_bt(low, out_ref[...]).astype(BF16)
    attention_backward(q_ref, own_ref, peer_ref, probs_ref, context_grad_ref, dq_ref, own_out, peer_out)


def project_back(dq_ref, dkv_ref, arrived_ref, mid_ref, weight_ref, proj_ref, sums_ref):
    width = dq_ref.shape[1]
    dq = dq_ref[...]
    dkv = (dkv_ref[...] + arrived_ref[...].astype(F32)).astype(BF16)
    proj_ref[:, :width] = dq
    proj_ref[:, width:] = dkv
    sums_ref[0:1, :] = total(dq.astype(F32))
    sums_ref[1:2, :] = total(dkv[:, width:].astype(F32))
    return mid_ref[...] + dot_bt(proj_ref[...], weight_ref[...])


def between_kernel(
    layer,
    dq_ref, dkv_ref, arrived_ref, mid_ref, unit_ref, inverse_ref, slope_ref, ffn_gain_ref,
    qkv_any, up_any, down_any,
    proj_ref, proj_sums_ref, down_low_ref, up_low_ref, grad_normed_ref, sums_ref,
    qkv_ref, up_ref, down_ref, sems,
):
    fetch_next = Fetch(layer + 1, [(qkv_any, qkv_ref)], sems)
    fetch = Fetch(layer, [(up_any, up_ref), (down_any, down_ref)], sems.at[pl.ds(1, 2)])
    fetch_next.wait(0)
    upstream = project_back(dq_ref, dkv_ref, arrived_ref, mid_ref, qkv_ref, proj_ref, proj_sums_ref)
    fetch.wait(0, 1)
    ffn_step_back(
        layer, upstream, unit_ref[...], inverse_ref[...], ffn_gain_ref, up_ref, down_ref, slope_ref,
        down_low_ref, up_low_ref, grad_normed_ref, sums_ref,
    )


def last_kernel(
    dq_ref, dkv_ref, arrived_ref, mid_ref, masked_ref, qkv_any,
    proj_ref, own_out, send_out, sums_ref,
    qkv_ref, sems,
):
    fetch = Fetch(0, [(qkv_any, qkv_ref)], sems)
    fetch.wait(0)
    upstream = project_back(dq_ref, dkv_ref, arrived_ref, mid_ref, qkv_ref, proj_ref, sums_ref)
    masked = masked_ref[...]
    sums_ref[2:3, :] = total(upstream * masked)
    grad = upstream * (1.0 - masked)
    half = grad.shape[0] // 2
    own_out[...] = grad[:half]
    send_out[...] = grad[half:].astype(BF16)


def call(body, operands, hbm, outputs, scratch, dmas, flops):
    shapes = [jax.ShapeDtypeStruct(shape, kind) for shape, kind in outputs]
    moved = sum(a.size * a.dtype.itemsize for a in operands)
    moved += sum(s.size * s.dtype.itemsize for s in shapes)
    moved += sum(math.prod(shape) * 2 for shape in scratch)
    whole = pl.BlockSpec(memory_space=pltpu.VMEM)
    return pl.pallas_call(
        body,
        out_shape=shapes,
        in_specs=[whole] * len(operands) + [pl.BlockSpec(memory_space=pl.ANY)] * len(hbm),
        out_specs=[whole] * len(shapes),
        scratch_shapes=[pltpu.VMEM(shape, BF16) for shape in scratch] + [pltpu.SemaphoreType.DMA((dmas,))],
        compiler_params=pltpu.CompilerParams(vmem_limit_bytes=48 * 2**20),
        cost_estimate=pl.CostEstimate(flops=flops, bytes_accessed=moved, transcendentals=0),
    )(*operands, *hbm)


def swap_seq(value, bit):
    count = lax.axis_size("seq")
    return lax.ppermute(value, "seq", [(i, i ^ bit) for i in range(count)])


def swap_dp(value, bit):
    count = lax.axis_size("dp")
    return lax.ppermute(value, "dp", [(i, i ^ bit) for i in range(count)])


def both(own):
    return jnp.concatenate([own, swap_seq(own, 1)], axis=0)


def half_columns(matrix, index):
    half = matrix.shape[1] // 2
    return lax.dynamic_slice_in_dim(matrix, index * half, half, axis=1)


def weight_grad(inputs_both, upstream, core):
    own = half_columns(upstream, core)
    other = swap_seq(half_columns(upstream, 1 - core), 1)
    return dot_at(inputs_both, jnp.concatenate([own, other], axis=0)).astype(BF16)


def halve(block, axis, mine, swap):
    sent = lax.dynamic_index_in_dim(block, 1 - mine, axis, keepdims=False)
    kept = lax.dynamic_index_in_dim(block, mine, axis, keepdims=False)
    return (kept.astype(F32) + swap(sent).astype(F32)).astype(BF16)


def scatter_sum(matrix, place, order):
    dp = lax.axis_size("dp")
    x, dp_index = place
    bits = dp.bit_length() - 1
    share = matrix.shape[0] // dp // 2
    block = matrix.reshape((2,) * (bits + 1) + (share, matrix.shape[1]))
    left = list(range(bits - 1, -1, -1)) + ["x"]
    steps = {"x": ["x"], "y": [0], "z": list(range(1, bits))}
    for step in sum((steps[name] for name in order), []):
        axis = left.index(step)
        left.pop(axis)
        if step == "x":
            block = halve(block, axis, x, lambda v: swap_seq(v, 2))
        else:
            block = halve(block, axis, (dp_index >> step) & 1, lambda v: swap_dp(v, 1 << step))
    return block


def gather_share(block, x, core):
    other = swap_seq(block, 2)
    rows = jnp.where(x == 0, jnp.concatenate([block, other]), jnp.concatenate([other, block]))
    other = swap_seq(rows, 1)
    whole = jnp.where(
        core == 0, jnp.concatenate([rows, other], axis=1), jnp.concatenate([other, rows], axis=1)
    )
    return whole.astype(F32)


def sum_everywhere(block):
    for bit in (1, 2):
        block = block + swap_seq(block, bit)
    for bit in range(lax.axis_size("dp").bit_length() - 1):
        block = block + swap_dp(block, 1 << bit)
    return block


def per_device(
    tokens, lengths, centre_flags, cotangent, mask_vector, qkv_weight, qv_bias, out_weight, out_bias,
    attn_gain, attn_shift, up_weight, up_bias, down_weight, down_bias, ffn_gain, ffn_shift,
):
    seq, dp_index = lax.axis_index("seq"), lax.axis_index("dp")
    x, core = seq // 2, seq % 2
    place = (x, dp_index)
    stretch, width = tokens.shape[1:]
    layers, hidden_units = qkv_weight.shape[0], up_weight.shape[2]
    rows, keys, heads = 2 * stretch, 4 * stretch, width // HEAD

    def one_slot(array):
        own = lax.dynamic_index_in_dim(array, x, 0, keepdims=False)
        other = lax.dynamic_index_in_dim(array, 1 - x, 0, keepdims=False)
        return own, swap_seq(other, 2)

    def two_slots(own, other):
        return jnp.where(x == 0, jnp.stack([own, other]), jnp.stack([other, own]))

    tokens_own, tokens_recv = one_slot(tokens)
    flags = jnp.stack(one_slot(centre_flags))
    flags_peer = swap_seq(flags, 1)
    by_offset = jnp.stack([flags[0], flags_peer[0], flags[1], flags_peer[1]])
    ordered = jnp.take(by_offset, jnp.arange(4) ^ seq, axis=0).reshape(-1)
    padded = jnp.pad(ordered, (SPAN, SPAN))
    count = padded[0:keys]
    for offset in range(1, 2 * SPAN + 1):
        count = count + padded[offset : offset + keys]
    masked_all = (count > 0).astype(F32).reshape(4, stretch)
    masked = jnp.take(masked_all, jnp.stack([seq, seq ^ 2]), axis=0).reshape(-1, 1)

    slot_length = lax.dynamic_index_in_dim(lengths, x, 0, keepdims=False)
    offsets = jnp.arange(stretch, dtype=jnp.int32)
    positions = jnp.concatenate([offsets + stretch * (seq ^ k) for k in (0, 2, 1, 3)])
    keep = (positions < slot_length).astype(F32).reshape(-1, 1)

    f_rows, b_rows = ((rows, width), F32), ((rows, width), BF16)
    b_hidden, b_kv = ((rows, hidden_units), BF16), ((rows, 2 * width), BF16)
    column, sums = ((rows, 1), F32), ((8, width), F32)
    probs = ((heads, keys, rows), BF16)
    w_qkv, w_out, w_up, w_down = (w.shape[1:] for w in (qkv_weight, out_weight, up_weight, down_weight))
    dense = lambda *shapes: 2 * rows * sum(math.prod(s) for s in shapes)
    attention = 4 * rows * keys * width

    hidden, low, q, kv = call(
        first_kernel, [tokens_own, tokens_recv, masked, mask_vector[None], qv_bias], [qkv_weight],
        [f_rows, b_rows, b_rows, b_kv], [w_qkv], 1, dense(w_qkv),
    )
    saved = []
    for layer in range(layers - 1):
        peer = swap_seq(kv, 1)
        out = call(
            functools.partial(forward_kernel, layer),
            [q, kv, peer, keep, hidden, out_bias, attn_gain, attn_shift, up_bias, down_bias, ffn_gain,
             ffn_shift, qv_bias],
            [out_weight, up_weight, down_weight, qkv_weight],
            [probs, b_rows, f_rows, column, b_rows, b_hidden, b_hidden, f_rows, column, f_rows, b_rows, b_rows,
             b_kv],
            [w_out, w_up, w_down, w_qkv], 4, dense(w_out, w_up, w_down, w_qkv) + attention,
        )
        saved.append((low, q, kv, peer) + tuple(out[:9]))
        hidden, low, q, kv = out[9:]
    peer = swap_seq(kv, 1)
    last = layers - 1
    cot_own, cot_recv = one_slot(cotangent)
    (
        probs_saved, context, unit, inverse, ffn_in, act, final, down_low, up_low, grad_normed, ffn_sums,
    ) = call(
        functools.partial(turn_kernel, last),
        [q, kv, peer, keep, hidden, cot_own, cot_recv, out_bias, attn_gain, attn_shift, up_bias, down_bias,
         ffn_gain, ffn_shift],
        [out_weight, up_weight, down_weight],
        [probs, b_rows, f_rows, column, b_rows, b_hidden, f_rows, b_rows, b_hidden, f_rows, sums],
        [w_out, w_up, w_down, (rows, hidden_units)], 3, 2 * dense(w_up, w_down) + dense(w_out) + attention,
    )
    layer_out = two_slots(final[:stretch], swap_seq(final[stretch:], 2))

    matrices, vectors = [None] * layers, [None] * layers
    for layer in reversed(range(layers)):
        if layer < last:
            (
                low, q, kv, peer, probs_saved, context, unit, inverse, ffn_in, act, slope, unit_two, inverse_two,
            ) = saved[layer]
            proj, proj_sums, down_low, up_low, grad_normed, ffn_sums = call(
                functools.partial(between_kernel, layer),
                [dq, dkv, arrived, mid, unit_two, inverse_two, slope, ffn_gain],
                [qkv_weight, up_weight, down_weight],
                [((rows, 3 * width), BF16), sums, b_rows, b_hidden, f_rows, sums],
                [w_qkv, w_up, w_down], 3, dense(w_qkv, w_up, w_down),
            )
            matrices[layer + 1][0] = (above, proj)
            vectors[layer + 1].append(proj_sums[:2])
        mid, attended_low, dq, dkv, dkv_peer, attn_sums = call(
            functools.partial(attend_back_kernel, layer),
            [grad_normed, unit, inverse, attn_gain, q, kv, peer, probs_saved], [out_weight],
            [f_rows, b_rows, b_rows, ((rows, 2 * width), F32), b_kv, sums],
            [w_out, (rows, width)], 1, dense(w_out) + 2 * attention,
        )
        arrived = swap_seq(dkv_peer, 1)
        above = low
        matrices[layer] = [None, (context, attended_low), (ffn_in, up_low), (act, down_low)]
        vectors[layer] = [ffn_sums[: 3 + hidden_units // width], attn_sums[:3]]
    proj, own_grad, send_grad, proj_sums = call(
        last_kernel, [dq, dkv, arrived, mid, masked], [qkv_weight],
        [((rows, 3 * width), BF16), ((stretch, width), F32), ((stretch, width), BF16), sums],
        [w_qkv], 1, dense(w_qkv),
    )
    matrices[0][0] = (above, proj)
    vectors[0].append(proj_sums[:3])
    input_grad = two_slots(own_grad, swap_seq(send_grad, 2).astype(F32))

    shares = [None] * layers
    for layer in reversed(range(layers)):
        orders = ("xzy", "yxz", "yzx", "xzy") if layer % 2 else ("yzx", "xyz", "xzy", "yzx")
        shares[layer] = [
            scatter_sum(weight_grad(both(a), g, core), place, order)
            for (a, g), order in zip(matrices[layer], orders)
        ]

    total_rows = [block for terms in vectors for block in terms]
    summed = sum_everywhere(jnp.concatenate(total_rows, axis=0))
    parts, at = [], 0
    for block in total_rows:
        parts.append(summed[at : at + block.shape[0]])
        at += block.shape[0]

    def pick(which, first, count=1):
        grads = jnp.stack(
            [parts[3 * layer + which][first : first + count].reshape(-1) for layer in range(layers)]
        )
        share = grads.shape[1] // lax.axis_size("dp")
        return lax.dynamic_slice_in_dim(grads, dp_index * share, share, axis=1)

    share = width // lax.axis_size("dp")
    vector_grad = lax.dynamic_slice_in_dim(parts[2][2], dp_index * share, share, axis=0)
    query_value = jnp.stack([parts[3 * layer + 2][:2].reshape(-1) for layer in range(layers)])
    share = 2 * width // lax.axis_size("dp")
    query_value = lax.dynamic_slice_in_dim(query_value, dp_index * share, share, axis=1)
    qkv_grad, out_grad, up_grad, down_grad = (
        jnp.stack([gather_share(shares[layer][i], x, core) for layer in range(layers)]) for i in range(4)
    )
    return (
        layer_out, input_grad, vector_grad, qkv_grad, query_value, out_grad, pick(1, 2), pick(1, 0), pick(1, 1),
        up_grad, pick(0, 3, hidden_units // width), down_grad, pick(0, 2), pick(0, 0), pick(0, 1),
    )


def solution(mesh):
    rows = P("dp", "seq", None)
    placed = (rows, P("dp"), P("dp", "seq"), rows) + (P(),) * 13
    matrix, vector = P(None, "dp", None), P(None, "dp")
    return jax.shard_map(
        per_device,
        mesh=mesh,
        in_specs=placed,
        out_specs=(
            rows, rows, P("dp"), matrix, vector, matrix, vector, vector, vector,
            matrix, vector, matrix, vector, vector, vector,
        ),
        check_vma=False,
    )
```

time: 430 us -> 416 us (0.967)
  Pallas kernels: 0 us -> 71.7 us
  matrix products: 85.4 us -> 14.3 us
  waiting for transfers between devices: 149 us -> 189 us
  other arithmetic: 52 us -> 19.8 us
  local copies, waits for them, and re-layouts: 64.1 us -> 39.2 us
    pallas_call x0 -> x7, Pallas kernels: none -> 71.7 us  [call(): pl.pallas_call(body, out_shape=shapes, in_specs=[whole] * len(operands) +...]
    dot_general x28 -> x0, matrix products: 67.7 us -> none  [the longest x8 22.3 us: dot_bt(): lax.dot_general(a, b, (((1,), (1,)), ((), ())), preferred_element_type=F32)]
    ppermute x27, waiting for transfers between devices: 87 us -> 127 us  [swap_dp(): return lax.ppermute(value, 'dp', [(i, i ^ bit) for i in range(count)])]
    reduce_sum x13 -> x0, other arithmetic: 13.9 us -> none  [the longest x2 3.3 us: attend_forward(): row_total = jnp.sum(exp_scores, axis=-1, keepdims=True)]
    slice x22 -> x5, local copies, waits for them, and re-layouts: 12.9 us -> 0.04 us  [the longest x1 0.03 us: pick(): parts[3 * layer + which][first:first + count].reshape(-1)]
    unnamed x280 -> x120, local copies, waits for them, and re-layouts: 8.61 us -> 20.9 us
    reshape x16 -> x0, local copies, waits for them, and re-layouts: 12.2 us -> none  [the longest x14 12.1 us: per_device(): v.reshape(dp, -1)]
    convert_element_type x10 -> x1, other arithmetic: 8.75 us -> 0.02 us  [per_device(): keep = (positions < slot_length).astype(F32).reshape(-1, 1)]
  transfers between devices with their start and end apart: 83 -> 79, of which waited for: 33 -> 36; matrix products, arithmetic and copies ran while one was open for 39% -> 12% of each run, Pallas kernels for 0% -> 13%
where the time goes in v2:
time: 416 us; the launch traced here: 408 us
  waiting for transfers between devices  189 us (45%)
  Pallas kernels  71.7 us (17%)
  starting transfers between devices  71.4 us (17%)
  local copies, waits for them, and re-layouts  39.2 us (9%)
  other arithmetic  19.8 us (5%)
  matrix products  14.3 us (3%)
    ppermute x27, waiting for transfers between devices, swap_dp(): return lax.ppermute(value, 'dp', [(i, i ^ bit) for i in range(count)])  127 us
    pallas_call x7, Pallas kernels, call(): pl.pallas_call(body, out_shape=shapes, in_specs=[whole] * len(operands) +...  71.7 us
    ppermute x52, waiting for transfers between devices, swap_seq(): return lax.ppermute(value, 'seq', [(i, i ^ bit) for i in range(count)])  62.7 us
    ppermute x52, starting transfers between devices, swap_seq(): return lax.ppermute(value, 'seq', [(i, i ^ bit) for i in range(count)])  37 us
    ppermute x27, starting transfers between devices, swap_dp(): return lax.ppermute(value, 'dp', [(i, i ^ bit) for i in range(count)])  34.4 us
    unnamed x120, local copies, waits for them, and re-layouts  20.9 us
    dot_general x8, matrix products, dot_at(): lax.dot_general(a, b, (((0,), (0,)), ((), ())), preferred_element_type=F32)  14.3 us
  transfers between devices with their start and end apart: 79, of which 36 were waited for; matrix products, arithmetic and copies ran while one was open for 12% of the time, Pallas kernels for 13%

profile of v2, /device:TPU:0, one launch (start us, length us, event | category | flops | bytes accessed | tf_op | source)
XLA Modules:
  0.0 407.8 jit_solution(4699559145194916984)
XLA Ops:
  1.7 3.0 collective-permute-start
  5.6 4.1 collective-permute-done.1
  13.1 3.2 shard_map.280
  25.4 15.9 %shard_map.281 = (bf16[12,512,256]{2,1,0:T(8,128)(2,1)}, bf16[256,768]{1,0:T(8,128)(2,1)S(1)}, f32[256,768]{1,0:T(8,128)S(1)}, f32[256,1]{1,0:T(8,128)S(1)}, bf1...) custom-call(bf16[256,768]{1,0:T(8,128)(2,1)S(1)} %get-tuple-element., ...), custom_call_target="tpu_custom_call" | custom-call | flops 4026531840 | bytes 27996160 | tf_op jit(solution)/shard_map/pallas_call | solution.py:331
  49.4 4.7 %collective-permute-done.5.cot_recv_ref = bf16[128,768]{1,0:T(8,128)(2,1)S(1)} collective-permute-done((bf16[128,768]{1,0:T(8,128)(2,1)S(1)}, bf16[128,768]{1,0:T(8,128)(2,1)S(1)}, u32[]{:S(2)}, u32[]{:S(2)}) %collective-permute-start.5) | collective-permute-done | bytes 196640 | tf_op jit(solution)/shard_map/ppermute | solution.py:344
  59.6 17.2 %shard_map.282 = (bf16[12,512,256]{2,1,0:T(8,128)(2,1)}, bf16[256,768]{1,0:T(8,128)(2,1)S(1)}, f32[256,768]{1,0:T(8,128)S(1)}, f32[256,1]{1,0:T(8,128)S(1)}, bf1...) custom-call(bf16[256,768]{1,0:T(8,128)(2,1)S(1)} %copy-done.9, ...), custom_call_target="tpu_custom_call" | custom-call | flops 5536481280 | bytes 25254912 | tf_op jit(solution)/shard_map/pallas_call | solution.py:331
  78.5 10.6 %shard_map.283 = (f32[256,768]{1,0:T(8,128)S(1)}, bf16[256,768]{1,0:T(8,128)(2,1)S(1)}, bf16[256,768]{1,0:T(8,128)(2,1)S(1)}, f32[256,1536]{1,0:T(8,128)}, bf16[...) custom-call(f32[256,768]{1,0:T(8,128)S(1)} %get-tuple-element.72.grad_ref, f32[256,768]{1,0:T(8,128)S(1)} %get-tuple-element.73.unit_ref, ...), custom_call_target="tpu_custom_call" | custom-call | flops 1107296256 | bytes 12221440 | tf_op jit(solution)/shard_map/pallas_call | solution.py:331
  96.9 6.4 %collective-permute-done.6 = f32[128,768]{1,0:T(8,128)S(1)} collective-permute-done((f32[128,768]{1,0:T(8,128)S(1)}, f32[128,768]{1,0:T(8,128)S(1)}, u32[]{:S(2)}, u32[]{:S(2)}) %collective-permute-start.6) | collective-permute-done | bytes 393248 | tf_op jit(solution)/shard_map/ppermute | solution.py:344
  105.1 10.9 %shard_map.284 = (bf16[256,2304]{1,0:T(8,128)(2,1)S(1)}, f32[8,768]{1,0:T(8,128)S(1)}, bf16[256,768]{1,0:T(8,128)(2,1)S(1)}, bf16[256,3072]{1,0:T(8,128)(2,1)}, ...) custom-call(bf16[256,768]{1,0:T(8,128)(2,1)S(1)} %get-tuple-element.76.dq_ref, f32[256,1536]{1,0:T(8,128)} %get-tuple-element.77.dkv_ref, ...), custom_call_target="tpu_custom_call" | custom-call | flops 3321888768 | bytes 22862848 | tf_op jit(solution)/shard_map/pallas_call | solution.py:331
  126.7 10.6 %shard_map.285 = (f32[256,768]{1,0:T(8,128)S(1)}, bf16[256,768]{1,0:T(8,128)(2,1)S(1)}, bf16[256,768]{1,0:T(8,128)(2,1)S(1)}, f32[256,1536]{1,0:T(8,128)}, bf16[...) custom-call(f32[256,768]{1,0:T(8,128)S(1)} %get-tuple-element.83.grad_ref, f32[256,768]{1,0:T(8,128)S(1)} %copy-done.14, ...), custom_call_target="tpu_custom_call" | custom-call | flops 1107296256 | bytes 12221440 | tf_op jit(solution)/shard_map/pallas_call | solution.py:331
  151.9 3.7 collective-permute-done.33
  163.1 3.0 collective-permute-done.35
  172.3 3.2 shard_map.286
  178.2 2.7 convolution_convert_fusion.3
  183.2 3.7 convolution_convert_fusion
  190.4 6.8 %collective-permute-done.11 = f32[25,768]{1,0:T(8,128)S(1)} collective-permute-done((f32[25,768]{1,0:T(8,128)S(1)}, f32[25,768]{1,0:T(8,128)S(1)}, u32[]{:S(2)}, u32[]{:S(2)}) %collective-permute-start.11) | collective-permute-done | bytes 76832 | tf_op jit(solution)/shard_map/ppermute | solution.py:344
  199.6 32.0 %collective-permute-done.12 = f32[25,768]{1,0:T(8,128)S(1)} collective-permute-done((f32[25,768]{1,0:T(8,128)S(1)}, f32[25,768]{1,0:T(8,128)S(1)}, u32[]{:S(2)}, u32[]{:S(2)}) %collective-permute-start.12) | collective-permute-done | bytes 76832 | tf_op jit(solution)/shard_map/ppermute | solution.py:349
  233.6 4.4 %collective-permute-done.13 = f32[25,768]{1,0:T(8,128)S(1)} collective-permute-done((f32[25,768]{1,0:T(8,128)S(1)}, f32[25,768]{1,0:T(8,128)S(1)}, u32[]{:S(2)}, u32[]{:S(2)}) %collective-permute-start.13) | collective-permute-done | bytes 76832 | tf_op jit(solution)/shard_map/ppermute | solution.py:349
  238.0 2.7 collective-permute-start.14
  259.4 9.3 %collective-permute-done.58 = bf16[2,2,48,1536]{3,2,1,0:T(8,128)(2,1)S(1)} collective-permute-done((bf16[2,2,48,1536]{3,2,1,0:T(8,128)(2,1)S(1)}, bf16[2,2,48,1536]{3,2,1,0:T(8,128)(2,1)S(1)}, u32[]{:S(2)}, u32[]{:S(2)}) %collective-permute-start.58) | collective-permute-done | bytes 589856 | tf_op jit(solution)/shard_map/ppermute | solution.py:349
  269.0 21.2 %collective-permute-done.26 = bf16[2,2,48,1152]{3,2,1,0:T(8,128)(2,1)S(1)} collective-permute-done((bf16[2,2,48,1152]{3,2,1,0:T(8,128)(2,1)S(1)}, bf16[2,2,48,1152]{3,2,1,0:T(8,128)(2,1)S(1)}, u32[]{:S(2)}, u32[]{:S(2)}) %collective-permute-start.26) | collective-permute-done | bytes 442400 | tf_op jit(solution)/shard_map/ppermute | solution.py:349
  296.3 6.6 %collective-permute-done.49 = bf16[2,2,2,48,1536]{4,3,2,0,1:T(8,128)(2,1)S(1)} collective-permute-done((bf16[2,2,2,48,1536]{4,3,2,0,1:T(8,128)(2,1)S(1)}, bf16[2,2,2,48,1536]{4,3,2,0,1:T(8,128)(2,1)S(1)}, u32[]{:S(2)}, u32[]{:S(2)}) %collective-permute-start.49) | collective-permute-done | bytes 1179680 | tf_op jit(solution)/shard_map/ppermute | solution.py:344
  303.5 13.5 %collective-permute-done.59 = bf16[2,48,1536]{2,1,0:T(8,128)(2,1)S(1)} collective-permute-done((bf16[2,48,1536]{2,1,0:T(8,128)(2,1)S(1)}, bf16[2,48,1536]{2,1,0:T(8,128)(2,1)S(1)}, u32[]{:S(2)}, u32[]{:S(2)}) %collective-permute-start.59) | collective-permute-done | bytes 294944 | tf_op jit(solution)/shard_map/ppermute | solution.py:349
  317.4 4.4 %collective-permute-done.27 = bf16[2,48,1152]{2,1,0:T(8,128)(2,1)S(1)} collective-permute-done((bf16[2,48,1152]{2,1,0:T(8,128)(2,1)S(1)}, bf16[2,48,1152]{2,1,0:T(8,128)(2,1)S(1)}, u32[]{:S(2)}, u32[]{:S(2)}) %collective-permute-start.27) | collective-permute-done | bytes 221216 | tf_op jit(solution)/shard_map/ppermute | solution.py:349
  323.2 4.1 %collective-permute-done.60 = bf16[48,1536]{1,0:T(8,128)(2,1)S(1)} collective-permute-done((bf16[48,1536]{1,0:T(8,128)(2,1)S(1)}, bf16[48,1536]{1,0:T(8,128)(2,1)S(1)}, u32[]{:S(2)}, u32[]{:S(2)}) %collective-permute-start.60) | collective-permute-done | bytes 147488 | tf_op jit(solution)/shard_map/ppermute | solution.py:344
  328.8 3.3 collective-permute-done.28
  338.8 3.7 collective-permute-done.68
  344.0 4.9 %collective-permute-done.69 = bf16[192,384]{1,0:T(8,128)(2,1)S(1)} collective-permute-done((bf16[192,384]{1,0:T(8,128)(2,1)S(1)}, bf16[192,384]{1,0:T(8,128)(2,1)S(1)}, u32[]{:S(2)}, u32[]{:S(2)}) %collective-permute-start.69) | collective-permute-done | bytes 147488 | tf_op jit(solution)/shard_map/ppermute | solution.py:344
  353.5 3.5 collective-permute-done.18
  357.3 20.8 %collective-permute-done.75 = bf16[2,192,384]{2,1,0:T(8,128)(2,1)S(1)} collective-permute-done((bf16[2,192,384]{2,1,0:T(8,128)(2,1)S(1)}, bf16[2,192,384]{2,1,0:T(8,128)(2,1)S(1)}, u32[]{:S(2)}, u32[]{:S(2)}) %collective-permute-start.75) | collective-permute-done | bytes 294944 | tf_op jit(solution)/shard_map/ppermute | solution.py:349
  379.6 4.7 %collective-permute-done.51 = bf16[2,48,1536]{2,1,0:T(8,128)(2,1)S(1)} collective-permute-done((bf16[2,48,1536]{2,1,0:T(8,128)(2,1)S(1)}, bf16[2,48,1536]{2,1,0:T(8,128)(2,1)S(1)}, u32[]{:S(2)}, u32[]{:S(2)}) %collective-permute-start.51) | collective-permute-done | bytes 294944 | tf_op jit(solution)/shard_map/ppermute | solution.py:349
  397.6 3.5 collective-permute-done.21
  (410 shorter events, 153.2 us)
Async XLA Ops:
  48.9 100.6 %collective-permute-start.63 = (bf16[256,3072]{1,0:T(8,128)(2,1)}, bf16[256,3072]{1,0:T(8,128)(2,1)S(1)}, u32[]{:S(2)}, u32[]{:S(2)}) collective-permute-start(bf16[256,3072]{1,0:T(8,128)(2,1)} %get-tuple-element.111), channel_id=1, source_target_pairs={{0,1},{1,0},{2,3},{3,2},{4,5},{5,4},{6,7},{7,6},{8,9},{9,8},{10,11... | collective-permute-start | bytes 4718600 | tf_op jit(solution)/shard_map/ppermute | solution.py:344
  48.9 127.1 %collective-permute-start.47 = (bf16[256,768]{1,0:T(8,128)(2,1)}, bf16[256,768]{1,0:T(8,128)(2,1)}, u32[]{:S(2)}, u32[]{:S(2)}) collective-permute-start(bf16[256,768]{1,0:T(8,128)(2,1)} %copy-done.40), channel_id=1, source_target_pairs={{0,1},{1,0},{2,3},{3,2},{4,5},{5,4},{6,7},{7,6},{8,9},{9,8},{10,11... | collective-permute-start | bytes 1179656 | tf_op jit(solution)/shard_map/ppermute | solution.py:344
  77.4 16.3 %collective-permute-start.39 = (bf16[256,768]{1,0:T(8,128)(2,1)S(1)}, bf16[256,768]{1,0:T(8,128)(2,1)S(1)}, u32[]{:S(2)}, u32[]{:S(2)}) collective-permute-start(bf16[256,768]{1,0:T(8,128)(2,1)S(1)} %get-tuple-element.105), channel_id=1, source_target_pairs={{0,1},{1,0},{2,3},{3,2},{4,5},{5,4},{6,7},{7,6},{8,9},{9,8},{10,11... | collective-permute-start | bytes 1179656 | tf_op jit(solution)/shard_map/ppermute | solution.py:344
  89.1 15.8 %collective-permute-start.7 = (bf16[256,1536]{1,0:T(8,128)(2,1)S(1)}, bf16[256,1536]{1,0:T(8,128)(2,1)S(1)}, u32[]{:S(2)}, u32[]{:S(2)}) collective-permute-start(bf16[256,1536]{1,0:T(8,128)(2,1)S(1)} %get-tuple-element.78), channel_id=1, source_target_pairs={{0,1},{1,0},{2,3},{3,2},{4,5},{5,4},{6,7},{7,6},{8,9},{9,8},{10,11... | collective-permute-start | bytes 2359304 | tf_op jit(solution)/shard_map/ppermute | solution.py:344
  103.3 39.0 %collective-permute-start.31 = (bf16[256,768]{1,0:T(8,128)(2,1)S(1)}, bf16[256,768]{1,0:T(8,128)(2,1)S(1)}, u32[]{:S(2)}, u32[]{:S(2)}) collective-permute-start(bf16[256,768]{1,0:T(8,128)(2,1)S(1)} %copy-done.45), channel_id=1, source_target_pairs={{0,1},{1,0},{2,3},{3,2},{4,5},{5,4},{6,7},{7,6},{8,9},{9,8},{10,11... | collective-permute-start | bytes 1179656 | tf_op jit(solution)/shard_map/ppermute | solution.py:344
  104.3 14.5 %collective-permute-start.56 = (bf16[256,1536]{1,0:T(8,128)(2,1)S(1)}, bf16[256,1536]{1,0:T(8,128)(2,1)S(1)}, u32[]{:S(2)}, u32[]{:S(2)}) collective-permute-start(bf16[256,1536]{1,0:T(8,128)(2,1)S(1)} %get-tuple-element.130), channel_id=1, source_target_pairs={{0,1},{1,0},{2,3},{3,2},{4,5},{5,4},{6,7},{7,6},{8,9},{9,8},{10,11... | collective-permute-start | bytes 2359304 | tf_op jit(solution)/shard_map/ppermute | solution.py:344
  105.0 13.4 %collective-permute-start.55 = (bf16[256,768]{1,0:T(8,128)(2,1)S(1)}, bf16[256,768]{1,0:T(8,128)(2,1)S(1)}, u32[]{:S(2)}, u32[]{:S(2)}) collective-permute-start(bf16[256,768]{1,0:T(8,128)(2,1)S(1)} %get-tuple-element.109), channel_id=1, source_target_pairs={{0,1},{1,0},{2,3},{3,2},{4,5},{5,4},{6,7},{7,6},{8,9},{9,8},{10,11... | collective-permute-start | bytes 1179656 | tf_op jit(solution)/shard_map/ppermute | solution.py:344
  118.4 42.9 %collective-permute-start.23 = (bf16[256,768]{1,0:T(8,128)(2,1)S(1)}, bf16[256,768]{1,0:T(8,128)(2,1)S(1)}, u32[]{:S(2)}, u32[]{:S(2)}) collective-permute-start(bf16[256,768]{1,0:T(8,128)(2,1)S(1)} %copy-done.43), channel_id=1, source_target_pairs={{0,1},{1,0},{2,3},{3,2},{4,5},{5,4},{6,7},{7,6},{8,9},{9,8},{10,11... | collective-permute-start | bytes 1179656 | tf_op jit(solution)/shard_map/ppermute | solution.py:344
  160.0 23.2 %collective-permute-start.71 = (bf16[256,3072]{1,0:T(8,128)(2,1)}, bf16[256,3072]{1,0:T(8,128)(2,1)}, u32[]{:S(2)}, u32[]{:S(2)}) collective-permute-start(bf16[256,3072]{1,0:T(8,128)(2,1)} %get-tuple-element.113), channel_id=1, source_target_pairs={{0,1},{1,0},{2,3},{3,2},{4,5},{5,4},{6,7},{7,6},{8,9},{9,8},{10,11... | collective-permute-start | bytes 4718600 | tf_op jit(solution)/shard_map/ppermute | solution.py:344
  161.0 16.8 %collective-permute-start.48 = (bf16[256,1536]{1,0:T(8,128)(2,1)}, bf16[256,1536]{1,0:T(8,128)(2,1)}, u32[]{:S(2)}, u32[]{:S(2)}) collective-permute-start(bf16[256,1536]{1,0:T(8,128)(2,1)} %get-tuple-element.128), channel_id=1, source_target_pairs={{0,1},{1,0},{2,3},{3,2},{4,5},{5,4},{6,7},{7,6},{8,9},{9,8},{10,11... | collective-permute-start | bytes 2359304 | tf_op jit(solution)/shard_map/ppermute | solution.py:344
  171.1 79.8 %collective-permute-start.15 = (bf16[256,768]{1,0:T(8,128)(2,1)S(1)}, bf16[256,768]{1,0:T(8,128)(2,1)}, u32[]{:S(2)}, u32[]{:S(2)}) collective-permute-start(bf16[256,768]{1,0:T(8,128)(2,1)S(1)} %copy-done.39), channel_id=1, source_target_pairs={{0,1},{1,0},{2,3},{3,2},{4,5},{5,4},{6,7},{7,6},{8,9},{9,8},{10,11... | collective-permute-start | bytes 1179656 | tf_op jit(solution)/shard_map/ppermute | solution.py:344
  176.1 74.5 %collective-permute-start.57 = (bf16[2,2,2,48,1536]{4,3,2,0,1:T(8,128)(2,1)}, bf16[2,2,2,48,1536]{4,3,2,0,1:T(8,128)(2,1)S(1)}, u32[]{:S(2)}, u32[]{:S(2)}) collective-permute-start(bf16[2,2,2,48,1536]{4,3,2,0,1:T(8,128)(2,1)} %bitcast.321), channel_id=1, source_target_pairs={{0,4},{4,0},{8,12},{12,8},{16,20},{20,16},{24,28},{28,24},{1,5},{5... | collective-permute-start | bytes 3538952 | tf_op jit(solution)/shard_map/ppermute | solution.py:349
  177.8 77.3 %collective-permute-start.65 = (bf16[2,2,2,192,384]{4,3,2,0,1:T(8,128)(2,1)}, bf16[2,2,2,192,384]{4,3,2,0,1:T(8,128)(2,1)S(1)}, u32[]{:S(2)}, u32[]{:S(2)}) collective-permute-start(bf16[2,2,2,192,384]{4,3,2,0,1:T(8,128)(2,1)} %bitcast.322), channel_id=1, source_target_pairs={{0,4},{4,0},{8,12},{12,8},{16,20},{20,16},{24,28},{28,24},{1,5},{5... | collective-permute-start | bytes 3538952 | tf_op jit(solution)/shard_map/ppermute | solution.py:349
  188.2 45.1 %collective-permute-start.9 = (bf16[128,768]{1,0:T(8,128)(2,1)S(1)}, bf16[128,768]{1,0:T(8,128)(2,1)S(1)}, u32[]{:S(2)}, u32[]{:S(2)}) collective-permute-start(bf16[128,768]{1,0:T(8,128)(2,1)S(1)} %get-tuple-element.92), channel_id=1, source_target_pairs={{0,2},{1,3},{2,0},{3,1},{4,6},{5,7},{6,4},{7,5},{8,10},{9,11},{10,... | collective-permute-start | bytes 589832 | tf_op jit(solution)/shard_map/ppermute | solution.py:344
  197.2 34.4 %collective-permute-start.12 = (f32[25,768]{1,0:T(8,128)S(1)}, f32[25,768]{1,0:T(8,128)S(1)}, u32[]{:S(2)}, u32[]{:S(2)}) collective-permute-start(f32[25,768]{1,0:T(8,128)S(1)} %add.425), channel_id=1, source_target_pairs={{0,4},{4,0},{8,12},{12,8},{16,20},{20,16},{24,28},{28,24},{1,5},{5... | collective-permute-start | bytes 230408 | tf_op jit(solution)/shard_map/ppermute | solution.py:349
  231.6 25.4 %collective-permute-start.25 = (bf16[2,2,2,48,1152]{4,3,2,0,1:T(8,128)(2,1)S(1)}, bf16[2,2,2,48,1152]{4,3,2,0,1:T(8,128)(2,1)S(1)}, u32[]{:S(2)}, u32[]{:S(2)}) collective-permute-start(bf16[2,2,2,48,1152]{4,3,2,0,1:T(8,128)(2,1)S(1)} %bitcast.329), channel_id=1, source_target_pairs={{0,2},{1,3},{2,0},{3,1},{4,6},{5,7},{6,4},{7,5},{8,10},{9,11},{10,... | collective-permute-start | bytes 2654216 | tf_op jit(solution)/shard_map/ppermute | solution.py:344
  244.2 49.3 %collective-permute-start.73 = (bf16[2,2,2,192,384]{4,3,2,0,1:T(8,128)(2,1)S(1)}, bf16[2,2,2,192,384]{4,3,2,0,1:T(8,128)(2,1)S(1)}, u32[]{:S(2)}, u32[]{:S(2)}) collective-permute-start(bf16[2,2,2,192,384]{4,3,2,0,1:T(8,128)(2,1)S(1)} %bitcast.324), channel_id=1, source_target_pairs={{0,2},{1,3},{2,0},{3,1},{4,6},{5,7},{6,4},{7,5},{8,10},{9,11},{10,... | collective-permute-start | bytes 3538952 | tf_op jit(solution)/shard_map/ppermute | solution.py:344
  250.9 52.0 %collective-permute-start.49 = (bf16[2,2,2,48,1536]{4,3,2,0,1:T(8,128)(2,1)S(1)}, bf16[2,2,2,48,1536]{4,3,2,0,1:T(8,128)(2,1)S(1)}, u32[]{:S(2)}, u32[]{:S(2)}) collective-permute-start(bf16[2,2,2,48,1536]{4,3,2,0,1:T(8,128)(2,1)S(1)} %bitcast.323), channel_id=1, source_target_pairs={{0,2},{1,3},{2,0},{3,1},{4,6},{5,7},{6,4},{7,5},{8,10},{9,11},{10,... | collective-permute-start | bytes 3538952 | tf_op jit(solution)/shard_map/ppermute | solution.py:344
  252.6 16.2 %collective-permute-start.58 = (bf16[2,2,48,1536]{3,2,1,0:T(8,128)(2,1)S(1)}, bf16[2,2,48,1536]{3,2,1,0:T(8,128)(2,1)S(1)}, u32[]{:S(2)}, u32[]{:S(2)}) collective-permute-start(bf16[2,2,48,1536]{3,2,1,0:T(8,128)(2,1)S(1)} %dynamic-slice_bitcast_fusion.2), channel_id=1, source_target_pairs={{0,8},{4,12},{8,0},{12,4},{16,24},{20,28},{24,16},{28,20},{1,9},{5... | collective-permute-start | bytes 1769480 | tf_op jit(solution)/shard_map/ppermute | solution.py:349
  255.1 78.4 %collective-permute-start.17 = (bf16[2,2,2,48,1152]{4,3,2,0,1:T(8,128)(2,1)S(1)}, bf16[2,2,2,48,1152]{4,3,2,0,1:T(8,128)(2,1)S(1)}, u32[]{:S(2)}, u32[]{:S(2)}) collective-permute-start(bf16[2,2,2,48,1152]{4,3,2,0,1:T(8,128)(2,1)S(1)} %bitcast.330), channel_id=1, source_target_pairs={{0,4},{4,0},{8,12},{12,8},{16,20},{20,16},{24,28},{28,24},{1,5},{5... | collective-permute-start | bytes 2654216 | tf_op jit(solution)/shard_map/ppermute | solution.py:349
  257.1 35.6 %collective-permute-start.66 = (bf16[2,2,192,384]{3,2,1,0:T(8,128)(2,1)S(1)}, bf16[2,2,192,384]{3,2,1,0:T(8,128)(2,1)S(1)}, u32[]{:S(2)}, u32[]{:S(2)}) collective-permute-start(bf16[2,2,192,384]{3,2,1,0:T(8,128)(2,1)S(1)} %dynamic-slice_bitcast_fusion.1), channel_id=1, source_target_pairs={{0,8},{4,12},{8,0},{12,4},{16,24},{20,28},{24,16},{28,20},{1,9},{5... | collective-permute-start | bytes 1769480 | tf_op jit(solution)/shard_map/ppermute | solution.py:349
  268.8 21.4 %collective-permute-start.26 = (bf16[2,2,48,1152]{3,2,1,0:T(8,128)(2,1)S(1)}, bf16[2,2,48,1152]{3,2,1,0:T(8,128)(2,1)S(1)}, u32[]{:S(2)}, u32[]{:S(2)}) collective-permute-start(bf16[2,2,48,1152]{3,2,1,0:T(8,128)(2,1)S(1)} %dynamic-slice_bitcast_fusion.4), channel_id=1, source_target_pairs={{0,8},{4,12},{8,0},{12,4},{16,24},{20,28},{24,16},{28,20},{1,9},{5... | collective-permute-start | bytes 1327112 | tf_op jit(solution)/shard_map/ppermute | solution.py:349
  290.2 26.8 %collective-permute-start.59 = (bf16[2,48,1536]{2,1,0:T(8,128)(2,1)S(1)}, bf16[2,48,1536]{2,1,0:T(8,128)(2,1)S(1)}, u32[]{:S(2)}, u32[]{:S(2)}) collective-permute-start(bf16[2,48,1536]{2,1,0:T(8,128)(2,1)S(1)} %dynamic-slice_bitcast_fusion.8), channel_id=1, source_target_pairs={{0,16},{4,20},{8,24},{12,28},{16,0},{20,4},{24,8},{28,12},{1,17},{... | collective-permute-start | bytes 884744 | tf_op jit(solution)/shard_map/ppermute | solution.py:349
  292.7 29.1 %collective-permute-start.27 = (bf16[2,48,1152]{2,1,0:T(8,128)(2,1)S(1)}, bf16[2,48,1152]{2,1,0:T(8,128)(2,1)S(1)}, u32[]{:S(2)}, u32[]{:S(2)}) collective-permute-start(bf16[2,48,1152]{2,1,0:T(8,128)(2,1)S(1)} %dynamic-slice_bitcast_fusion.10), channel_id=1, source_target_pairs={{0,16},{4,20},{8,24},{12,28},{16,0},{20,4},{24,8},{28,12},{1,17},{... | collective-permute-start | bytes 663560 | tf_op jit(solution)/shard_map/ppermute | solution.py:349
  293.6 40.9 %collective-permute-start.67 = (bf16[2,192,384]{2,1,0:T(8,128)(2,1)S(1)}, bf16[2,192,384]{2,1,0:T(8,128)(2,1)S(1)}, u32[]{:S(2)}, u32[]{:S(2)}) collective-permute-start(bf16[2,192,384]{2,1,0:T(8,128)(2,1)S(1)} %dynamic-slice_bitcast_fusion.7), channel_id=1, source_target_pairs={{0,16},{4,20},{8,24},{12,28},{16,0},{20,4},{24,8},{28,12},{1,17},{... | collective-permute-start | bytes 884744 | tf_op jit(solution)/shard_map/ppermute | solution.py:349
  302.9 46.0 %collective-permute-start.74 = (bf16[2,2,192,384]{3,2,1,0:T(8,128)(2,1)S(1)}, bf16[2,2,192,384]{3,2,1,0:T(8,128)(2,1)S(1)}, u32[]{:S(2)}, u32[]{:S(2)}) collective-permute-start(bf16[2,2,192,384]{3,2,1,0:T(8,128)(2,1)S(1)} %dynamic-slice_bitcast_fusion), channel_id=1, source_target_pairs={{0,8},{4,12},{8,0},{12,4},{16,24},{20,28},{24,16},{28,20},{1,9},{5... | collective-permute-start | bytes 1769480 | tf_op jit(solution)/shard_map/ppermute | solution.py:349
  317.0 32.7 %collective-permute-start.50 = (bf16[2,2,48,1536]{3,2,1,0:T(8,128)(2,1)S(1)}, bf16[2,2,48,1536]{3,2,1,0:T(8,128)(2,1)S(1)}, u32[]{:S(2)}, u32[]{:S(2)}) collective-permute-start(bf16[2,2,48,1536]{3,2,1,0:T(8,128)(2,1)S(1)} %dynamic-slice_bitcast_fusion.3), channel_id=1, source_target_pairs={{0,8},{4,12},{8,0},{12,4},{16,24},{20,28},{24,16},{28,20},{1,9},{5... | collective-permute-start | bytes 1769480 | tf_op jit(solution)/shard_map/ppermute | solution.py:349
  334.5 22.6 %collective-permute-start.18 = (bf16[2,2,48,1152]{3,2,1,0:T(8,128)(2,1)S(1)}, bf16[2,2,48,1152]{3,2,1,0:T(8,128)(2,1)S(1)}, u32[]{:S(2)}, u32[]{:S(2)}) collective-permute-start(bf16[2,2,48,1152]{3,2,1,0:T(8,128)(2,1)S(1)} %dynamic-slice_bitcast_fusion.5), channel_id=1, source_target_pairs={{0,8},{4,12},{8,0},{12,4},{16,24},{20,28},{24,16},{28,20},{1,9},{5... | collective-permute-start | bytes 1327112 | tf_op jit(solution)/shard_map/ppermute | solution.py:349
  349.0 37.0 %collective-permute-start.70 = (bf16[384,384]{1,0:T(8,128)(2,1)S(1)}, bf16[384,384]{1,0:T(8,128)(2,1)S(1)}, u32[]{:S(2)}, u32[]{:S(2)}) collective-permute-start(bf16[384,384]{1,0:T(8,128)(2,1)S(1)} %maximum_select_fusion.10), channel_id=1, source_target_pairs={{0,1},{1,0},{2,3},{3,2},{4,5},{5,4},{6,7},{7,6},{8,9},{9,8},{10,11... | collective-permute-start | bytes 884744 | tf_op jit(solution)/shard_map/ppermute | solution.py:344
  349.8 28.3 %collective-permute-start.75 = (bf16[2,192,384]{2,1,0:T(8,128)(2,1)S(1)}, bf16[2,192,384]{2,1,0:T(8,128)(2,1)S(1)}, u32[]{:S(2)}, u32[]{:S(2)}) collective-permute-start(bf16[2,192,384]{2,1,0:T(8,128)(2,1)S(1)} %dynamic-slice_bitcast_fusion.6), channel_id=1, source_target_pairs={{0,16},{4,20},{8,24},{12,28},{16,0},{20,4},{24,8},{28,12},{1,17},{... | collective-permute-start | bytes 884744 | tf_op jit(solution)/shard_map/ppermute | solution.py:349
  350.8 33.6 %collective-permute-start.51 = (bf16[2,48,1536]{2,1,0:T(8,128)(2,1)S(1)}, bf16[2,48,1536]{2,1,0:T(8,128)(2,1)S(1)}, u32[]{:S(2)}, u32[]{:S(2)}) collective-permute-start(bf16[2,48,1536]{2,1,0:T(8,128)(2,1)S(1)} %dynamic-slice_bitcast_fusion.9), channel_id=1, source_target_pairs={{0,16},{4,20},{8,24},{12,28},{16,0},{20,4},{24,8},{28,12},{1,17},{... | collective-permute-start | bytes 884744 | tf_op jit(solution)/shard_map/ppermute | solution.py:349
  357.2 31.0 %collective-permute-start.19 = (bf16[2,48,1152]{2,1,0:T(8,128)(2,1)S(1)}, bf16[2,48,1152]{2,1,0:T(8,128)(2,1)S(1)}, u32[]{:S(2)}, u32[]{:S(2)}) collective-permute-start(bf16[2,48,1152]{2,1,0:T(8,128)(2,1)S(1)} %dynamic-slice_bitcast_fusion.11), channel_id=1, source_target_pairs={{0,16},{4,20},{8,24},{12,28},{16,0},{20,4},{24,8},{28,12},{1,17},{... | collective-permute-start | bytes 663560 | tf_op jit(solution)/shard_map/ppermute | solution.py:349
  (104 other events, 550.6 us)
